TPU v7x, 32 devices: a whole 2x2x4 slice. The times are simulated.
32 devices in a mesh: wide: 8 (over z, y), narrow: 4 (over x, core).
Axes of the slice: x: 2, y: 2, z: 4, core: 2. Of those that a mesh axis runs over, the one named last changes fastest.
Arguments:
- tokens: bfloat16 [32768, 768], P(('wide', 'narrow')), may hold values from -6 to 6
- cotangent: bfloat16 [32768, 768], P(('wide', 'narrow')), may hold values from -6 to 6
- lengths: int32 [64], P(('wide', 'narrow')), may hold values from 1 to 512, as said below
- buckets: int32 [32], P(('wide', 'narrow')), may hold values from 0 to 2, as said below
- w_query: bfloat16 [768, 768], P(('wide', 'narrow')), may hold values from -0.21875 to 0.21875
- w_key: bfloat16 [768, 768], P(('wide', 'narrow')), may hold values from -0.21875 to 0.21875
- w_value: bfloat16 [768, 768], P(('wide', 'narrow')), may hold values from -0.21875 to 0.21875
- w_output: bfloat16 [768, 768], P(('wide', 'narrow')), may hold values from -0.875 to 0.875
- b_query: bfloat16 [768], P(('wide', 'narrow')), may hold values from -3 to 3
- b_value: bfloat16 [768], P(('wide', 'narrow')), may hold values from -3 to 3
- b_output: bfloat16 [768], P(('wide', 'narrow')), may hold values from -3 to 3
- gain_attn: bfloat16 [768], P(('wide', 'narrow')), may hold values from 0.5 to 1.5
- shift_attn: bfloat16 [768], P(('wide', 'narrow')), may hold values from -2 to 2
- w_inner: bfloat16 [768, 3072], P(('wide', 'narrow')), may hold values from -0.21875 to 0.21875
- b_inner: bfloat16 [3072], P(('wide', 'narrow')), may hold values from -3 to 3
- w_outer: bfloat16 [3072, 768], P(('wide', 'narrow')), may hold values from -0.109375 to 0.109375
- b_outer: bfloat16 [768], P(('wide', 'narrow')), may hold values from -3 to 3
- gain_ffn: bfloat16 [768], P(('wide', 'narrow')), may hold values from 0.5 to 1.5
- shift_ffn: bfloat16 [768], P(('wide', 'narrow')), may hold values from -2 to 2
Outputs:
- layer_out: bfloat16 [32768, 768], P(('wide', 'narrow'))
- grad_tokens: bfloat16 [32768, 768], P(('wide', 'narrow'))
- grad_w_query: float32 [768, 768], P(('wide', 'narrow'))
- grad_w_key: float32 [768, 768], P(('wide', 'narrow'))
- grad_w_value: float32 [768, 768], P(('wide', 'narrow'))
- grad_w_output: float32 [768, 768], P(('wide', 'narrow'))
- grad_b_query: float32 [768], P(('wide', 'narrow'))
- grad_b_value: float32 [768], P(('wide', 'narrow'))
- grad_b_output: float32 [768], P(('wide', 'narrow'))
- grad_gain_attn: float32 [768], P(('wide', 'narrow'))
- grad_shift_attn: float32 [768], P(('wide', 'narrow'))
- grad_w_inner: float32 [768, 3072], P(('wide', 'narrow'))
- grad_b_inner: float32 [3072], P(('wide', 'narrow'))
- grad_w_outer: float32 [3072, 768], P(('wide', 'narrow'))
- grad_b_outer: float32 [768], P(('wide', 'narrow'))
- grad_gain_ffn: float32 [768], P(('wide', 'narrow'))
- grad_shift_ffn: float32 [768], P(('wide', 'narrow'))
Inputs may be any that keep to these rules, and one draw needn't show every extreme that they name: `lengths`: some sequence has length 512 in every draw. `buckets`: some device has bucket 2 in every draw.
All inputs are finite; a program needn't handle non-finite values.
Results may differ from a plain program's by a relative error of at most 0.014.
Values may be sent and summed in bfloat16 or wider, within the bound.
No kernel may reach another device: no remote copies, remote signals or barrier semaphores. Data moves between devices by JAX's collectives and lax.ppermute only.
A program may use at most 192 MiB of HBM per device.

v0:
```python
from functools import partial

import jax
import jax.numpy as jnp
from jax import lax
from jax.sharding import PartitionSpec as P

D = 768
H = 12
HD = 64
BLEN = 128
MAXLEN = 512
SEQ_DEV = 2


EPSILON = 1e-12
HALF_ROOT = 0.7071067811865476
DENSITY = 0.3989422804014327


def product(left_side, right_side):
    return jnp.dot(left_side, right_side, preferred_element_type=jnp.float32)


def left_product(left_side, right_side):
    return lax.dot_general(
        left_side, right_side, (((0,), (0,)), ((), ())), preferred_element_type=jnp.float32
    )


def right_product(left_side, right_side):
    return lax.dot_general(
        left_side, right_side, (((1,), (1,)), ((), ())), preferred_element_type=jnp.float32
    )


def column_sum(matrix):
    return jnp.sum(matrix.astype(jnp.float32), axis=0)


def norm_rows(hidden, gain, shift):
    center = hidden - jnp.mean(hidden, axis=1, keepdims=True)
    scaling = lax.rsqrt(jnp.mean(center * center, axis=1, keepdims=True) + EPSILON)
    normed = center * scaling
    return (normed * gain + shift, normed, scaling)


def norm_back(upstream, normed, scaling, gain):
    inner = upstream * gain
    back = scaling * (
        inner
        - jnp.mean(inner, axis=1, keepdims=True)
        - normed * jnp.mean(inner * normed, axis=1, keepdims=True)
    )
    return (back, jnp.sum(upstream * normed, axis=0), jnp.sum(upstream, axis=0))


def gelu_slope(values):
    return (
        0.5 * (1.0 + lax.erf(values * HALF_ROOT))
        + values * jnp.exp(-0.5 * values * values) * DENSITY
    )


def attn_weights(
    w_query, w_key, w_value, w_output, b_query, b_value, b_output, gain_attn, shift_attn
):
    gathered = (
        lax.all_gather(w_query, ("wide", "narrow"), axis=0, tiled=True),
        lax.all_gather(w_key, ("wide", "narrow"), axis=0, tiled=True),
        lax.all_gather(w_value, ("wide", "narrow"), axis=0, tiled=True),
        lax.all_gather(w_output, ("wide", "narrow"), axis=0, tiled=True),
        lax.all_gather(b_query, ("wide", "narrow"), axis=0, tiled=True),
        lax.all_gather(b_value, ("wide", "narrow"), axis=0, tiled=True),
        lax.all_gather(b_output, ("wide", "narrow"), axis=0, tiled=True),
        lax.all_gather(gain_attn, ("wide", "narrow"), axis=0, tiled=True),
        lax.all_gather(shift_attn, ("wide", "narrow"), axis=0, tiled=True),
    )
    return gathered


def ffn_weights(w_inner, b_inner, w_outer, b_outer, gain_ffn, shift_ffn):
    gathered = (
        lax.all_gather(w_inner, ("wide", "narrow"), axis=0, tiled=True),
        lax.all_gather(b_inner, ("wide", "narrow"), axis=0, tiled=True),
        lax.all_gather(w_outer, ("wide", "narrow"), axis=0, tiled=True),
        lax.all_gather(b_outer, ("wide", "narrow"), axis=0, tiled=True),
        lax.all_gather(gain_ffn, ("wide", "narrow"), axis=0, tiled=True),
        lax.all_gather(shift_ffn, ("wide", "narrow"), axis=0, tiled=True),
    )
    return gathered


def attn_reduce(
    query_grad,
    key_grad,
    value_grad,
    output_grad,
    bias_query,
    bias_value,
    bias_output,
    gain_grad,
    shift_grad,
):
    owned = (
        lax.psum_scatter(query_grad, ("wide", "narrow"), scatter_dimension=0, tiled=True),
        lax.psum_scatter(key_grad, ("wide", "narrow"), scatter_dimension=0, tiled=True),
        lax.psum_scatter(value_grad, ("wide", "narrow"), scatter_dimension=0, tiled=True),
        lax.psum_scatter(output_grad, ("wide", "narrow"), scatter_dimension=0, tiled=True),
        lax.psum_scatter(bias_query, ("wide", "narrow"), scatter_dimension=0, tiled=True),
        lax.psum_scatter(bias_value, ("wide", "narrow"), scatter_dimension=0, tiled=True),
        lax.psum_scatter(bias_output, ("wide", "narrow"), scatter_dimension=0, tiled=True),
        lax.psum_scatter(gain_grad, ("wide", "narrow"), scatter_dimension=0, tiled=True),
        lax.psum_scatter(shift_grad, ("wide", "narrow"), scatter_dimension=0, tiled=True),
    )
    return owned


def ffn_reduce(inner_grad, bias_inner, outer_grad, bias_outer, gain_grad, shift_grad):
    owned = (
        lax.psum_scatter(inner_grad, ("wide", "narrow"), scatter_dimension=0, tiled=True),
        lax.psum_scatter(bias_inner, ("wide", "narrow"), scatter_dimension=0, tiled=True),
        lax.psum_scatter(outer_grad, ("wide", "narrow"), scatter_dimension=0, tiled=True),
        lax.psum_scatter(bias_outer, ("wide", "narrow"), scatter_dimension=0, tiled=True),
        lax.psum_scatter(gain_grad, ("wide", "narrow"), scatter_dimension=0, tiled=True),
        lax.psum_scatter(shift_grad, ("wide", "narrow"), scatter_dimension=0, tiled=True),
    )
    return owned


def masked_scores(query_heads, key_heads, seq_length, key_span):
    scaled = jnp.einsum(
        "qhd,khd->hqk", query_heads, key_heads, preferred_element_type=jnp.float32
    ) * HD ** (-0.5)
    places = jnp.arange(key_span, dtype=jnp.int32)
    key_limit = jnp.minimum(seq_length, key_span)
    return jnp.where((places < key_limit)[None, None, :], scaled, -1e30)


def heads_forward(key_span, query_block, key_block, value_block, lengths):

    def one_sequence(items):
        query_part, key_part, value_part, seq_length = items
        query_heads = query_part.reshape(MAXLEN, H, HD)
        key_heads = key_part.reshape(key_span, H, HD)
        value_heads = value_part.reshape(key_span, H, HD)
        scores = masked_scores(query_heads, key_heads, seq_length, key_span)
        row_max = jnp.max(scores, axis=2, keepdims=True)
        powers = jnp.exp(scores - row_max)
        row_sum = jnp.sum(powers, axis=2, keepdims=True)
        weights = (powers / row_sum).astype(jnp.bfloat16)
        attended = jnp.einsum(
            "hqk,khd->qhd", weights, value_heads, preferred_element_type=jnp.float32
        )
        return (attended.reshape(MAXLEN, D), (row_max + jnp.log(row_sum))[:, :, 0])

    return lax.map(
        one_sequence, (query_block, key_block[:, :key_span], value_block[:, :key_span], lengths)
    )


def heads_backward(key_span, query_block, key_block, value_block, grad_block, log_sums, lengths):
    scaling = HD ** (-0.5)

    def one_sequence(items):
        query_part, key_part, value_part, grad_part, seq_lse, seq_length = items
        query_heads = query_part.reshape(MAXLEN, H, HD)
        key_heads = key_part.reshape(key_span, H, HD)
        value_heads = value_part.reshape(key_span, H, HD)
        grad_heads = grad_part.reshape(MAXLEN, H, HD)
        scores = masked_scores(query_heads, key_heads, seq_length, key_span)
        weights = jnp.exp(scores - seq_lse[:, :, None])
        rounded = weights.astype(jnp.bfloat16)
        value_grad = jnp.einsum(
            "hqk,qhd->khd", rounded, grad_heads, preferred_element_type=jnp.float32
        )
        weight_grad = jnp.einsum(
            "qhd,khd->hqk", grad_heads, value_heads, preferred_element_type=jnp.float32
        )
        score_grad = (
            weights * (weight_grad - jnp.sum(weight_grad * weights, axis=2, keepdims=True))
        ).astype(jnp.bfloat16)
        query_grad = (
            jnp.einsum("hqk,khd->qhd", score_grad, key_heads, preferred_element_type=jnp.float32)
            * scaling
        )
        key_grad = (
            jnp.einsum("hqk,qhd->khd", score_grad, query_heads, preferred_element_type=jnp.float32)
            * scaling
        )
        padding = ((0, MAXLEN - key_span), (0, 0))
        return (
            query_grad.reshape(MAXLEN, D).astype(jnp.bfloat16),
            jnp.pad(key_grad.reshape(key_span, D), padding).astype(jnp.bfloat16),
            jnp.pad(value_grad.reshape(key_span, D), padding).astype(jnp.bfloat16),
        )

    return lax.map(
        one_sequence,
        (
            query_block,
            key_block[:, :key_span],
            value_block[:, :key_span],
            grad_block,
            log_sums,
            lengths,
        ),
    )


def body(
    tokens,
    cotangent,
    lengths,
    buckets,
    w_query,
    w_key,
    w_value,
    w_output,
    b_query,
    b_value,
    b_output,
    gain_attn,
    shift_attn,
    w_inner,
    b_inner,
    w_outer,
    b_outer,
    gain_ffn,
    shift_ffn,
):
    attn_full = attn_weights(
        w_query, w_key, w_value, w_output, b_query, b_value, b_output, gain_attn, shift_attn
    )
    q_full, k_full, v_full, o_full, bq_full, bv_full, bo_full, gain_one, shift_one = attn_full
    queries = (product(tokens, q_full) + bq_full.astype(jnp.float32)).astype(jnp.bfloat16)
    key_rows = product(tokens, k_full).astype(jnp.bfloat16)
    value_rows = (product(tokens, v_full) + bv_full.astype(jnp.float32)).astype(jnp.bfloat16)
    query_block = queries.reshape(SEQ_DEV, MAXLEN, D)
    key_block = key_rows.reshape(SEQ_DEV, MAXLEN, D)
    value_block = value_rows.reshape(SEQ_DEV, MAXLEN, D)
    bucket_now = buckets[0]
    spans = [BLEN, 2 * BLEN, 4 * BLEN]
    head_out, head_lse = lax.switch(
        bucket_now,
        [partial(heads_forward, key_span) for key_span in spans],
        query_block,
        key_block,
        value_block,
        lengths,
    )
    attended = head_out.reshape(SEQ_DEV * MAXLEN, D).astype(jnp.bfloat16)
    first_sum = tokens.astype(jnp.float32) + product(attended, o_full) + bo_full.astype(jnp.float32)
    normed, unit_one, scale_one = norm_rows(
        first_sum, gain_one.astype(jnp.float32), shift_one.astype(jnp.float32)
    )
    ffn_full = ffn_weights(w_inner, b_inner, w_outer, b_outer, gain_ffn, shift_ffn)
    inner_full, bi_full, outer_full, bout_full, gain_two, shift_two = ffn_full
    normed_low = normed.astype(jnp.bfloat16)
    hidden = product(normed_low, inner_full) + bi_full.astype(jnp.float32)
    active = jax.nn.gelu(hidden, approximate=False).astype(jnp.bfloat16)
    second_sum = normed + product(active, outer_full) + bout_full.astype(jnp.float32)
    layer_out, unit_two, scale_two = norm_rows(
        second_sum, gain_two.astype(jnp.float32), shift_two.astype(jnp.float32)
    )
    ffn_back = ffn_weights(w_inner, b_inner, w_outer, b_outer, gain_ffn, shift_ffn)
    inner_back, _, outer_back, _, gain_back_two, _ = ffn_back
    second_grad, gain_two_grad, shift_two_grad = norm_back(
        cotangent.astype(jnp.float32), unit_two, scale_two, gain_back_two.astype(jnp.float32)
    )
    branch_grad = second_grad.astype(jnp.bfloat16)
    outer_grad = left_product(active, branch_grad)
    bout_grad = column_sum(branch_grad)
    hidden_grad = (right_product(branch_grad, outer_back) * gelu_slope(hidden)).astype(jnp.bfloat16)
    inner_grad = left_product(normed_low, hidden_grad)
    bi_grad = column_sum(hidden_grad)
    ffn_owned = ffn_reduce(
        inner_grad, bi_grad, outer_grad, bout_grad, gain_two_grad, shift_two_grad
    )
    normed_grad = second_grad + right_product(hidden_grad, inner_back)
    attn_back = attn_weights(
        w_query, w_key, w_value, w_output, b_query, b_value, b_output, gain_attn, shift_attn
    )
    q_back, k_back, v_back, o_back, _, _, _, gain_back_one, _ = attn_back
    first_grad, gain_one_grad, shift_one_grad = norm_back(
        normed_grad, unit_one, scale_one, gain_back_one.astype(jnp.float32)
    )
    first_low = first_grad.astype(jnp.bfloat16)
    output_grad = left_product(attended, first_low)
    bo_grad = column_sum(first_low)
    attended_grad = right_product(first_low, o_back).astype(jnp.bfloat16)
    head_q, head_k, head_v = lax.switch(
        bucket_now,
        [partial(heads_backward, key_span) for key_span in spans],
        query_block,
        key_block,
        value_block,
        attended_grad.reshape(SEQ_DEV, MAXLEN, D),
        head_lse,
        lengths,
    )
    query_grad = head_q.reshape(SEQ_DEV * MAXLEN, D)
    key_grad = head_k.reshape(SEQ_DEV * MAXLEN, D)
    value_grad = head_v.reshape(SEQ_DEV * MAXLEN, D)
    attn_owned = attn_reduce(
        left_product(tokens, query_grad),
        left_product(tokens, key_grad),
        left_product(tokens, value_grad),
        output_grad,
        column_sum(query_grad),
        column_sum(value_grad),
        bo_grad,
        gain_one_grad,
        shift_one_grad,
    )
    grad_tokens = (
        first_grad
        + right_product(query_grad, q_back)
        + right_product(key_grad, k_back)
        + right_product(value_grad, v_back)
    ).astype(jnp.bfloat16)
    return (
        layer_out.astype(jnp.bfloat16),
        grad_tokens,
        attn_owned[0],
        attn_owned[1],
        attn_owned[2],
        attn_owned[3],
        attn_owned[4],
        attn_owned[5],
        attn_owned[6],
        attn_owned[7],
        attn_owned[8],
        ffn_owned[0],
        ffn_owned[1],
        ffn_owned[2],
        ffn_owned[3],
        ffn_owned[4],
        ffn_owned[5],
    )


def solution(mesh):
    placed = (
        P(("wide", "narrow"), None),
        P(("wide", "narrow"), None),
        P(("wide", "narrow")),
        P(("wide", "narrow")),
        P(("wide", "narrow"), None),
        P(("wide", "narrow"), None),
        P(("wide", "narrow"), None),
        P(("wide", "narrow"), None),
        P(("wide", "narrow")),
        P(("wide", "narrow")),
        P(("wide", "narrow")),
        P(("wide", "narrow")),
        P(("wide", "narrow")),
        P(("wide", "narrow"), None),
        P(("wide", "narrow")),
        P(("wide", "narrow"), None),
        P(("wide", "narrow")),
        P(("wide", "narrow")),
        P(("wide", "narrow")),
    )
    return jax.shard_map(
        body,
        mesh=mesh,
        in_specs=placed,
        out_specs=(
            P(("wide", "narrow"), None),
            P(("wide", "narrow"), None),
            P(("wide", "narrow"), None),
            P(("wide", "narrow"), None),
            P(("wide", "narrow"), None),
            P(("wide", "narrow"), None),
            P(("wide", "narrow")),
            P(("wide", "narrow")),
            P(("wide", "narrow")),
            P(("wide", "narrow")),
            P(("wide", "narrow")),
            P(("wide", "narrow"), None),
            P(("wide", "narrow")),
            P(("wide", "narrow"), None),
            P(("wide", "narrow")),
            P(("wide", "narrow")),
            P(("wide", "narrow")),
        ),
        check_vma=False,
    )
```

profile of v0, /device:TPU:0, one launch (start us, length us, event | category | flops | bytes accessed | tf_op | source)
XLA Modules:
  0.0 1224.0 jit_solution(3867432494891424739)
XLA Ops:
  18.8 42.4 %all-reduce.23 = (bf16[768]{0:T(1024)(128)(2,1)S(1)}, bf16[768]{0:T(1024)(128)(2,1)S(1)}, bf16[768]{0:T(1024)(128)(2,1)S(1)}, bf16[768]{0:T(1024)(128)(2,1)S(1)}...) all-reduce(bf16[768]{0:T(1024)(128)(2,1)S(1)} %dynamic-update-slice, ...), channel_id=1, replica_groups=mesh['wide'=8,'narrow'=4] {'wide','narrow'}, use_global_device_ids=true, to_apply=%add.4 | all-reduce | flops 9216 | bytes 36864
  74.2 49.8 %all-gather.9.cloned.1.call-done = bf16[768,768]{1,0:T(8,128)(2,1)} async-done(((bf16[24,768]{1,0:T(8,128)(2,1)}), bf16[768,768]{1,0:T(8,128)(2,1)}) %all-gather.9.cloned.1.call-update) | async-done | bytes 1179664 | tf_op jit(solution)/shard_map/all_gather | solution.py:71
  127.8 52.1 %all-gather.11.cloned.1.call-done = bf16[768,768]{1,0:T(8,128)(2,1)} async-done(((bf16[24,768]{1,0:T(8,128)(2,1)}), bf16[768,768]{1,0:T(8,128)(2,1)}) %all-gather.11.cloned.1.call-update) | async-done | bytes 1179664 | tf_op jit(solution)/shard_map/all_gather | solution.py:69
  182.6 29.4 %conditional.2 = (bf16[2,512,768]{1,2,0:T(8,128)(2,1)}, f32[2,12,512]{2,1,0:T(8,128)}) conditional(s32[]{:T(128)} %bitcast.61, (bf16[2,512,768]{2,1,0:T(8,128)(2,1)}, bf16[2,512,768]{2,1,0:T(8,128)(2,1)}, s32[2]{0:T(128)S(1)}, bf16[2,512,768]{2,1,0:T(8,128)(2,1)S(1)}) %tuple.257, (bf16[2,512,768]{2,1,0:T(8,128)(2,1)}, ...), branch_computations={%region_0.5_spmd, %region_5.10_spmd, %region_10.15_spmd} | conditional | flops 843049472 | bytes 102656792 | solution.py:244
  188.0 10.8 while.76
  213.8 21.9 %all-gather.13.cloned.1.call-done = bf16[768,768]{1,0:T(8,128)(2,1)} async-done(((bf16[24,768]{1,0:T(8,128)(2,1)}), bf16[768,768]{1,0:T(8,128)(2,1)}) %all-gather.13.cloned.1.call-update) | async-done | bytes 1179664 | tf_op jit(solution)/shard_map/all_gather | solution.py:72
  241.2 59.8 %all-gather.15.cloned.1.call-done = bf16[768,3072]{1,0:T(8,128)(2,1)} async-done(((bf16[24,3072]{1,0:T(8,128)(2,1)}), bf16[768,3072]{1,0:T(8,128)(2,1)}) %all-gather.15.cloned.1.call-update) | async-done | bytes 4718608 | tf_op jit(solution)/shard_map/all_gather | solution.py:84
  301.0 38.8 %fusion.42 = (bf16[1024,3072]{1,0:T(8,128)(2,1)}, f32[1024,3072]{1,0:T(8,128)}) fusion(f32[3072]{0:T(1024)S(1)} %copy-done.73, bf16[768,3072]{1,0:T(8,128)(2,1)} %all-gather.15.cloned.1.call-done, f32[1024,768]{0,1:T(8,128)} %copy-done.11, f32[768]{0:T(1024)S(1)} %copy-done.75, f32[768]{0:T(1024)S(1)} %copy-done.64, f32[1024]{0:T(1024)S(1)} %add_rsqrt_fusion.1, ...), kind=kOutput, calls=%fused_computation.105 | convolution fusion | flops 5043388416 | bytes 26765312 | tf_op jit(solution)/shard_map/dot_general | solution.py:22
  339.8 26.5 %all-gather.17.cloned.1.call-done = bf16[3072,768]{1,0:T(8,128)(2,1)} async-done(((bf16[96,768]{1,0:T(8,128)(2,1)}), bf16[3072,768]{1,0:T(8,128)(2,1)}) %all-gather.17.cloned.1.call-update) | async-done | bytes 4718608 | tf_op jit(solution)/shard_map/all_gather | solution.py:86
  366.3 9.4 fusion.74
  382.3 14.7 %convert_reduce_fusion = (f32[3072]{0:T(1024)}, bf16[1024,3072]{1,0:T(8,128)(2,1)}) fusion(f32[1024,3072]{1,0:T(8,128)} %get-tuple-element.840, f32[3072]{0:T(1024)S(1)} %copy-done.73, bf16[1024,768]{0,1:T(8,128)(2,1)S(1)} %get-tuple-element.809, bf16[3072,768]{1,0:T(8,128)(2,1)S(1)} %copy-done.81), kind=kOutput, calls=%fused_computation.112 | convolution fusion | flops 4872729600 | bytes 25190400 | tf_op jit(solution)/shard_map/dot_general | solution.py:32
  397.1 9.8 multiply_reduce_fusion.3
  411.3 48.6 %conditional.3 = (bf16[2,512,768]{1,2,0:T(8,128)(2,1)}, bf16[2,512,768]{1,2,0:T(8,128)(2,1)}, bf16[2,512,768]{1,2,0:T(8,128)(2,1)}) conditional(s32[]{:T(128)} %bitcast.61, (bf16[2,512,768]{2,1,0:T(8,128)(2,1)}, bf16[2,512,768]{2,1,0:T(8,128)(2,1)}, s32[2]{0:T(128)S(1)}, bf16[2,512,768]{2,1,0:T(8,128)(2,1)S(1)}, ...), branch_computations={%region_23.27_spmd, %region_27.31_spmd, %region_31.35_spmd} | conditional | flops 2062412288 | bytes 179482112 | solution.py:292
  419.3 33.3 %while.79 = (s32[]{:T(128)}, bf16[2,512,768]{1,2,0:T(8,128)(2,1)}, bf16[2,512,768]{1,2,0:T(8,128)(2,1)}, bf16[2,512,768]{1,2,0:T(8,128)(2,1)}, bf16[2,128,768]{1...) while((s32[]{:T(128)}, bf16[2,512,768]{1,2,0:T(8,128)(2,1)}, ...), condition=%wide.region_26.26_spmd, body=%wide.region_24.25_spmd.sunk | while | flops 511469696 | bytes 92726512 | solution.py:198
  476.6 4.8 convolution_bitcast_fusion
  484.7 5.3 fusion.65
  490.1 10.5 fusion.68
  502.1 10.2 fusion.79
  515.7 95.5 %all-reduce.22 = (f32[768]{0:T(1024)S(1)}, f32[768]{0:T(1024)S(1)}, f32[768]{0:T(1024)S(1)}, f32[768]{0:T(1024)S(1)}, f32[768]{0:T(1024)S(1)}, /*index=5*/f32[30...) all-reduce(f32[768]{0:T(1024)S(1)} %convert_reduce_fusion.5, ...), channel_id=6, replica_groups=mesh['wide'=8,'narrow'=4] {'wide','narrow'}, use_global_device_ids=true, to_apply=%region_40.41.clone | all-reduce | flops 9216 | bytes 73728
  626.6 98.7 %reduce-scatter.21.cloned.1.call-done = f32[24,768]{1,0:T(8,128)} async-done(((f32[768,768]{1,0:T(8,128)}), f32[24,768]{1,0:T(8,128)}) %reduce-scatter.21.cloned.1.call-update) | async-done | bytes 73744
  725.3 103.9 %reduce-scatter.23.cloned.1.call-done = f32[24,768]{1,0:T(8,128)} async-done(((f32[768,768]{1,0:T(8,128)}), f32[24,768]{1,0:T(8,128)}) %reduce-scatter.23.cloned.1.call-update) | async-done | bytes 73744
  829.2 104.6 %reduce-scatter.13.cloned.1.call-done = f32[24,768]{1,0:T(8,128)} async-done(((f32[768,768]{1,0:T(8,128)}), f32[24,768]{1,0:T(8,128)}) %reduce-scatter.13.cloned.1.call-update) | async-done | bytes 73744 | tf_op jit(solution)/shard_map/reduce_scatter | solution.py:109
  933.8 141.1 %reduce-scatter.15.cloned.1.call-done = f32[24,3072]{1,0:T(8,128)} async-done(((f32[768,3072]{1,0:T(8,128)}), f32[24,3072]{1,0:T(8,128)}) %reduce-scatter.15.cloned.1.call-update) | async-done | bytes 294928 | tf_op jit(solution)/shard_map/reduce_scatter | solution.py:121
  1074.8 141.9 %reduce-scatter.17.cloned.1.call-done = f32[96,768]{1,0:T(8,128)} async-done(((f32[3072,768]{1,0:T(8,128)}), f32[96,768]{1,0:T(8,128)}) %reduce-scatter.17.cloned.1.call-update) | async-done | bytes 294928 | tf_op jit(solution)/shard_map/reduce_scatter | solution.py:123
  (329 shorter events, 142.6 us)
Async XLA Ops:
  7.2 61.0 %copy-start.47 = (bf16[1024,768]{1,0:T(8,128)(2,1)S(1)}, bf16[1024,768]{1,0:T(8,128)(2,1)}, u32[]{:S(2)}) copy-start(bf16[1024,768]{1,0:T(8,128)(2,1)} %param.38) | copy-start | bytes 4718596
  7.2 63.2 %all-gather.7.cloned.1.call-start = ((), (), s32[]{:S(2)}) async-start(), calls=%async_computation.6 | async-start | bytes 1216512 | tf_op jit(solution)/shard_map/all_gather | solution.py:70
  7.9 116.1 %all-gather.9.cloned.1.call-start = ((), (), s32[]{:S(2)}) async-start(), calls=%async_computation.7 | async-start | bytes 1216512 | tf_op jit(solution)/shard_map/all_gather | solution.py:71
  8.7 171.2 %all-gather.11.cloned.1.call-start = ((), (), s32[]{:S(2)}) async-start(), calls=%async_computation.8 | async-start | bytes 1216512 | tf_op jit(solution)/shard_map/all_gather | solution.py:69
  9.4 226.3 %all-gather.13.cloned.1.call-start = ((), (), s32[]{:S(2)}) async-start(), calls=%async_computation.9 | async-start | bytes 1216512 | tf_op jit(solution)/shard_map/all_gather | solution.py:72
  10.0 291.0 %all-gather.15.cloned.1.call-start = ((), (), s32[]{:S(2)}) async-start(), calls=%async_computation.10 | async-start | bytes 4866048 | tf_op jit(solution)/shard_map/all_gather | solution.py:84
  10.6 355.7 %all-gather.17.cloned.1.call-start = ((), (), s32[]{:S(2)}) async-start(), calls=%async_computation.11 | async-start | bytes 4866048 | tf_op jit(solution)/shard_map/all_gather | solution.py:86
  11.2 615.4 %reduce-scatter.19.cloned.1.call-start = ((), (), s32[]{:S(2)}) async-start(), calls=%async_computation.15 | async-start | bytes 2433024
  127.8 54.8 %copy-start.84 = (s32[2]{0:T(128)S(1)}, s32[2]{0:T(128)}, u32[]{:S(2)}) copy-start(s32[2]{0:T(128)} %param.39) | copy-start | bytes 28
  212.0 23.7 %copy-start.78 = (f32[768]{0:T(1024)S(1)}, f32[768]{0:T(1024)}, u32[]{:S(2)}) copy-start(f32[768]{0:T(1024)} %convert_element_type.250) | copy-start | bytes 9220
  213.8 25.4 %copy-start.50 = (bf16[2,512,768]{2,1,0:T(8,128)(2,1)}, bf16[2,512,768]{2,1,0:T(8,128)(2,1)S(1)}, u32[]{:S(2)}) copy-start(bf16[2,512,768]{2,1,0:T(8,128)(2,1)S(1)} %copy.152) | copy-start | bytes 4718596
  239.1 61.9 %copy-start.64 = (f32[768]{0:T(1024)S(1)}, f32[768]{0:T(1024)}, u32[]{:S(2)}) copy-start(f32[768]{0:T(1024)} %convert_element_type.251) | copy-start | bytes 9220
  239.1 61.9 %copy-start.73 = (f32[3072]{0:T(1024)S(1)}, f32[3072]{0:T(1024)}, u32[]{:S(2)}) copy-start(f32[3072]{0:T(1024)} %convert_element_type.254) | copy-start | bytes 36868
  239.2 61.9 %copy-start.75 = (f32[768]{0:T(1024)S(1)}, f32[768]{0:T(1024)}, u32[]{:S(2)}) copy-start(f32[768]{0:T(1024)} %convert_element_type.252) | copy-start | bytes 9220
  239.2 167.8 %copy-start.61 = (f32[1024]{0:T(1024)}, f32[1024]{0:T(1024)S(1)}, u32[]{:S(2)}) copy-start(f32[1024]{0:T(1024)S(1)} %broadcast_multiply_fusion.5) | copy-start | bytes 12292
  241.2 165.8 %copy-start.66 = (f32[1024]{0:T(1024)}, f32[1024]{0:T(1024)S(1)}, u32[]{:S(2)}) copy-start(f32[1024]{0:T(1024)S(1)} %add_rsqrt_fusion.1) | copy-start | bytes 12292
  241.2 125.1 %copy-start.77 = (f32[768]{0:T(1024)S(1)}, f32[768]{0:T(1024)}, u32[]{:S(2)}) copy-start(f32[768]{0:T(1024)} %convert_element_type.256) | copy-start | bytes 9220
  379.1 18.0 %slice-start.5 = ((s8[4718592]{0:T(1024)(128)(4,1)}), s8[4194304]{0:T(1024)(128)(4,1)S(1)}, s32[]{:S(2)}) async-start(s8[4718592]{0:T(1024)(128)(4,1)} %bitcast.398), calls=%async_computation.23 | async-start | bytes 8388608
  467.9 257.4 %reduce-scatter.21.cloned.1.call-start = ((), (), s32[]{:S(2)}) async-start(), calls=%async_computation.16 | async-start | bytes 2433024
  475.8 353.3 %reduce-scatter.23.cloned.1.call-start = ((), (), s32[]{:S(2)}) async-start(), calls=%async_computation.17 | async-start | bytes 2433024
  484.6 449.2 %reduce-scatter.13.cloned.1.call-start = ((), (), s32[]{:S(2)}) async-start(), calls=%async_computation.12 | async-start | bytes 2433024 | tf_op jit(solution)/shard_map/reduce_scatter | solution.py:109
  490.0 584.8 %reduce-scatter.15.cloned.1.call-start = ((), (), s32[]{:S(2)}) async-start(), calls=%async_computation.13 | async-start | bytes 9732096 | tf_op jit(solution)/shard_map/reduce_scatter | solution.py:121
  500.7 716.0 %reduce-scatter.17.cloned.1.call-start = ((), (), s32[]{:S(2)}) async-start(), calls=%async_computation.14 | async-start | bytes 9732096 | tf_op jit(solution)/shard_map/reduce_scatter | solution.py:123
  512.3 103.5 %copy-start.51 = (bf16[2,512,768]{2,1,0:T(8,128)(2,1)S(1)}, bf16[2,512,768]{2,1,0:T(8,128)(2,1)}, u32[]{:S(2)}) copy-start(bf16[2,512,768]{2,1,0:T(8,128)(2,1)} %copy.168) | copy-start | bytes 4718596
  (70 other events, 222.8 us)
Sparse Core Ops, SparseCore 0:
  10.9 56.9 all-gather.6
  70.8 53.1 all-gather.8
  126.9 52.9 all-gather.10
  182.7 52.9 all-gather.12
  238.4 62.5 all-gather.14
  303.8 62.4 all-gather.16
  468.0 152.3 reduce-scatter.18
  627.2 98.0 reduce-scatter.20
  731.1 97.9 reduce-scatter.22
  835.7 97.9 reduce-scatter.12
  940.3 134.5 reduce-scatter.14
  1082.2 134.4 reduce-scatter.16
where the time goes:
time: 1230 us; the launch traced here: 1220 us
  waiting for transfers between devices  804 us (65%)
  matrix products  147 us (12%)
  blocking collectives  138 us (11%)
  local copies, waits for them, and re-layouts  77.9 us (6%)
  loops' own time  23.8 us (2%)
  other arithmetic  17.2 us (1%)
  between operations  16 us (1%)
    unnamed x15, waiting for transfers between devices  206 us
    reduce_scatter x1, waiting for transfers between devices, ffn_reduce(): lax.psum_scatter(outer_grad, ('wide', 'narrow'), scatter_dimension=0, til...  142 us
    reduce_scatter x1, waiting for transfers between devices, ffn_reduce(): lax.psum_scatter(inner_grad, ('wide', 'narrow'), scatter_dimension=0, til...  141 us
    unnamed x2, blocking collectives  138 us
    reduce_scatter x1, waiting for transfers between devices, attn_reduce(): lax.psum_scatter(output_grad, ('wide', 'narrow'), scatter_dimension=0, ti...  105 us
    dot_general x6, matrix products, product(): return jnp.dot(left_side, right_side, preferred_element_type=jnp.float32)  61.9 us
    all_gather x1, waiting for transfers between devices, ffn_weights(): lax.all_gather(w_inner, ('wide', 'narrow'), axis=0, tiled=True)  59.8 us
    all_gather x1, waiting for transfers between devices, attn_weights(): lax.all_gather(w_query, ('wide', 'narrow'), axis=0, tiled=True)  52.1 us
  transfers between devices with their start and end apart: 12, of which 10 were waited for; matrix products, arithmetic and copies ran while one was open for 12% of the time, Pallas kernels for 0%

commit v1 on v0

v1 whole, which is shorter than its diff:
```python
from functools import partial

import jax
import jax.numpy as jnp
from jax import lax
from jax.experimental import pallas as pl
from jax.experimental.pallas import tpu as pltpu
from jax.sharding import PartitionSpec as P

D = 768
H = 12
HD = 64
FF = 3072
BLEN = 128
MAXLEN = 512
SEQ_DEV = 2
PAIR = 2 * HD
PAIRS = H // 2
CHUNKS = FF // D

EPSILON = 1e-12
DENSITY = 0.3989422804014327
LOG2E = 1.4426950408889634
SCORE_SCALE = LOG2E * HD ** (-0.5)
VMEM = 60 * 1024 * 1024
BF = jnp.bfloat16
F32 = jnp.float32


def params(**kw):
    return pltpu.CompilerParams(vmem_limit_bytes=VMEM, **kw)


def dot_nn(a, b):
    return lax.dot_general(a, b, (((1,), (0,)), ((), ())), preferred_element_type=F32)


def dot_nt(a, b):
    return lax.dot_general(a, b, (((1,), (1,)), ((), ())), preferred_element_type=F32)


def dot_tn(a, b):
    return lax.dot_general(a, b, (((0,), (0,)), ((), ())), preferred_element_type=F32)


def whole(shape):
    return pl.BlockSpec(shape, lambda *_: (0,) * len(shape), pipeline_mode=pl.Buffered(1))


def qkv_kernel(x_ref, w_ref, b_ref, out_ref):
    x = x_ref[...]
    for part in range(3):
        rows = dot_nn(x, w_ref[:, part * D : (part + 1) * D])
        out_ref[part] = (rows + b_ref[part : part + 1, :]).astype(BF)


def project_qkv(tokens, w_qkv, biases, rows=256):
    count = tokens.shape[0]
    return pl.pallas_call(
        qkv_kernel,
        grid=(count // rows,),
        in_specs=[
            pl.BlockSpec((rows, D), lambda i: (i, 0)),
            whole((D, 3 * D)),
            whole((8, D)),
        ],
        out_specs=pl.BlockSpec((3, rows, D), lambda i: (0, i, 0)),
        out_shape=jax.ShapeDtypeStruct((3, count, D), BF),
        compiler_params=params(),
        cost_estimate=pl.CostEstimate(
            flops=2 * count * D * 3 * D, bytes_accessed=8 * count * D + 6 * D * D, transcendentals=0
        ),
        name="project_qkv",
    )(tokens, w_qkv, biases)


def lane_half(shape):
    return lax.broadcasted_iota(jnp.int32, shape, 1) < HD


def live_rows(keys, limit):
    return lax.broadcasted_iota(jnp.int32, (keys, 1), 0) < limit


def pick_half(matrix, low, head):
    zero = jnp.zeros_like(matrix)
    return jnp.where(low, matrix, zero) if head == 0 else jnp.where(low, zero, matrix)


def forward_block(keys, limit, qkv_ref, out_ref, lse_ref):
    queries = qkv_ref[0]
    key_part = qkv_ref[1, :keys]
    value_t = qkv_ref[2, :keys].T
    low = lane_half((keys, PAIR))
    live = live_rows(keys, limit)
    outs = []
    for head in range(2):
        scores = dot_nt(pick_half(key_part, low, head), queries)
        scores = jnp.where(live, scores, -1e30)
        top = jnp.max(scores, axis=0, keepdims=True) * SCORE_SCALE
        powers = jnp.exp2(scores * SCORE_SCALE - top)
        total = jnp.sum(powers, axis=0, keepdims=True)
        mixed = dot_nn(value_t[head * HD : (head + 1) * HD], powers.astype(BF))
        outs.append(mixed / total)
        lse_ref[0, 0, head : head + 1, :] = top + jnp.log2(total)
    out_ref[...] = jnp.concatenate(outs, axis=0).T.astype(BF)


def backward_block(keys, limit, qkv_ref, grad_ref, lse_ref, out_ref):
    queries = qkv_ref[0]
    key_part = qkv_ref[1, :keys]
    value_part = qkv_ref[2, :keys]
    grads = grad_ref[...]
    key_t = key_part.T
    low = lane_half((keys, PAIR))
    live = live_rows(keys, limit)
    scaling = HD ** (-0.5)
    query_grads, key_grads, value_grads = [], [], []
    for head in range(2):
        scores = dot_nt(pick_half(key_part, low, head), queries)
        logits = scores * SCORE_SCALE - lse_ref[0, 0, head : head + 1, :]
        weights = jnp.exp2(jnp.where(live, logits, -1e30))
        value_grads.append(dot_nn(weights.astype(BF), grads))
        weight_grad = dot_nt(pick_half(value_part, low, head), grads)
        delta = jnp.sum(weight_grad * weights, axis=0, keepdims=True)
        score_grad = (weights * (weight_grad - delta)).astype(BF)
        key_grads.append(dot_nn(score_grad, queries))
        query_grads.append(dot_nn(key_t[head * HD : (head + 1) * HD], score_grad))
    out_ref[0] = (jnp.concatenate(query_grads, axis=0) * scaling).T.astype(BF)
    out_ref[1, :keys] = (jnp.where(low, key_grads[0], key_grads[1]) * scaling).astype(BF)
    out_ref[2, :keys] = jnp.where(low, value_grads[0], value_grads[1]).astype(BF)
    if keys < MAXLEN:
        out_ref[1, keys:] = jnp.zeros((MAXLEN - keys, PAIR), BF)
        out_ref[2, keys:] = jnp.zeros((MAXLEN - keys, PAIR), BF)


def by_blocks(block, limits_ref, *refs):
    limit = limits_ref[pl.program_id(0)]
    for blocks in range(1, MAXLEN // BLEN + 1):
        low_edge, high_edge = (blocks - 1) * BLEN, blocks * BLEN

        @pl.when((limit > low_edge) & (limit <= high_edge))
        def _():
            block(high_edge, limit, *refs)


def heads_forward(qkv, limits):
    count = qkv.shape[1]
    seqs = count // MAXLEN
    return pl.pallas_call(
        partial(by_blocks, forward_block),
        grid_spec=pltpu.PrefetchScalarGridSpec(
            num_scalar_prefetch=1,
            grid=(seqs, PAIRS),
            in_specs=[pl.BlockSpec((3, MAXLEN, PAIR), lambda s, p, _: (0, s, p))],
            out_specs=[
                pl.BlockSpec((MAXLEN, PAIR), lambda s, p, _: (s, p)),
                pl.BlockSpec((1, 1, 2, MAXLEN), lambda s, p, _: (s, p, 0, 0)),
            ],
        ),
        out_shape=[
            jax.ShapeDtypeStruct((count, D), BF),
            jax.ShapeDtypeStruct((seqs, PAIRS, 2, MAXLEN), F32),
        ],
        compiler_params=params(),
        cost_estimate=pl.CostEstimate(
            flops=16 * seqs * H * MAXLEN * MAXLEN * HD,
            bytes_accessed=8 * count * D,
            transcendentals=seqs * H * MAXLEN * MAXLEN,
        ),
        name="heads_forward",
    )(limits, qkv)


def heads_backward(qkv, grads, lse, limits):
    count = qkv.shape[1]
    seqs = count // MAXLEN
    return pl.pallas_call(
        partial(by_blocks, backward_block),
        grid_spec=pltpu.PrefetchScalarGridSpec(
            num_scalar_prefetch=1,
            grid=(seqs, PAIRS),
            in_specs=[
                pl.BlockSpec((3, MAXLEN, PAIR), lambda s, p, _: (0, s, p)),
                pl.BlockSpec((MAXLEN, PAIR), lambda s, p, _: (s, p)),
                pl.BlockSpec((1, 1, 2, MAXLEN), lambda s, p, _: (s, p, 0, 0)),
            ],
            out_specs=pl.BlockSpec((3, MAXLEN, PAIR), lambda s, p, _: (0, s, p)),
        ),
        out_shape=jax.ShapeDtypeStruct((3, count, D), BF),
        compiler_params=params(),
        cost_estimate=pl.CostEstimate(
            flops=40 * seqs * H * MAXLEN * MAXLEN * HD,
            bytes_accessed=14 * count * D,
            transcendentals=seqs * H * MAXLEN * MAXLEN,
        ),
        name="heads_backward",
    )(limits, qkv, grads, lse)


def normal_parts(hidden):
    size = jnp.abs(hidden)
    power = jnp.exp2(hidden * hidden * (-0.5 * LOG2E))
    t = 1.0 / (1.0 + 0.23164190 * size)
    series = t * (
        0.127414796
        + t * (-0.142248368 + t * (0.7107068705 + t * (-0.7265760135 + t * 0.5307027145)))
    )
    tail = series * power
    phi = jnp.where(hidden < 0.0, tail, 1.0 - tail)
    return phi, power


def row_mean(matrix):
    return jnp.mean(matrix, axis=1, keepdims=True)


def norm_rows(hidden):
    center = hidden - row_mean(hidden)
    scale = lax.rsqrt(row_mean(center * center) + EPSILON)
    return center * scale, scale


def norm_back(upstream, unit, scale, gain):
    inner = upstream * gain
    return scale * (inner - row_mean(inner) - unit * row_mean(inner * unit))


def fold_rows(matrix):
    rows, columns = matrix.shape
    return jnp.sum(matrix.reshape(rows // 8, 8, columns), axis=0)


BIAS_ROWS = ("b_query", "zero", "b_value", "b_output", "gain_attn", "shift_attn", "b_outer", "gain_ffn", "shift_ffn")


def ffn_kernel(
    tok_ref, att_ref, cot_ref, wo_ref, wi_ref, wout_ref, vec_ref, bi_ref,
    out_ref, nl_ref, act_ref, bg_ref, hg_ref, fl_ref, gf_ref, ag_ref, sums_ref, bisum_ref,
    slope_ref,
):
    vec = lambda name: vec_ref[BIAS_ROWS.index(name) : BIAS_ROWS.index(name) + 1, :]

    @pl.when(pl.program_id(0) == 0)
    def _():
        sums_ref[...] = jnp.zeros_like(sums_ref)
        bisum_ref[...] = jnp.zeros_like(bisum_ref)

    first = tok_ref[...].astype(F32) + dot_nn(att_ref[...], wo_ref[...]) + vec("b_output")
    unit_one, scale_one = norm_rows(first)
    normed = unit_one * vec("gain_attn") + vec("shift_attn")
    nl = normed.astype(BF)
    nl_ref[...] = nl
    second = normed + vec("b_outer")
    for c in range(CHUNKS):
        cols = slice(c * D, (c + 1) * D)
        hidden = dot_nn(nl, wi_ref[:, cols]) + bi_ref[:, cols]
        phi, power = normal_parts(hidden)
        active = (hidden * phi).astype(BF)
        slope_ref[:, cols] = phi + hidden * power * DENSITY
        act_ref[:, cols] = active
        second = second + dot_nn(active, wout_ref[cols, :])
    unit_two, scale_two = norm_rows(second)
    out_ref[...] = (unit_two * vec("gain_ffn") + vec("shift_ffn")).astype(BF)
    cot = cot_ref[...].astype(F32)
    sums_ref[0] += fold_rows(cot * unit_two)
    sums_ref[1] += fold_rows(cot)
    grad_second = norm_back(cot, unit_two, scale_two, vec("gain_ffn"))
    bg = grad_second.astype(BF)
    bg_ref[...] = bg
    sums_ref[2] += fold_rows(bg.astype(F32))
    grad_normed = grad_second
    for c in range(CHUNKS):
        cols = slice(c * D, (c + 1) * D)
        hg = (dot_nt(bg, wout_ref[cols, :]) * slope_ref[:, cols]).astype(BF)
        hg_ref[:, cols] = hg
        bisum_ref[:, cols] += fold_rows(hg.astype(F32))
        grad_normed = grad_normed + dot_nt(hg, wi_ref[:, cols])
    sums_ref[3] += fold_rows(grad_normed * unit_one)
    sums_ref[4] += fold_rows(grad_normed)
    grad_first = norm_back(grad_normed, unit_one, scale_one, vec("gain_attn"))
    gf_ref[...] = grad_first
    fl = grad_first.astype(BF)
    fl_ref[...] = fl
    sums_ref[5] += fold_rows(fl.astype(F32))
    ag_ref[...] = dot_nt(fl, wo_ref[...]).astype(BF)


def feed_forward(tokens, attended, cotangent, w_o, w_i, w_out, vecs, b_inner, rows=256):
    count = tokens.shape[0]
    narrow = pl.BlockSpec((rows, D), lambda i: (i, 0))
    wide = pl.BlockSpec((rows, FF), lambda i: (i, 0))
    shape = jax.ShapeDtypeStruct
    return pl.pallas_call(
        ffn_kernel,
        grid=(count // rows,),
        in_specs=[narrow, narrow, narrow, whole((D, D)), whole((D, FF)), whole((FF, D)), whole((16, D)), whole((1, FF))],
        out_specs=[narrow, narrow, wide, narrow, wide, narrow, narrow, narrow, whole((6, 8, D)), whole((8, FF))],
        out_shape=[
            shape((count, D), BF), shape((count, D), BF), shape((count, FF), BF), shape((count, D), BF),
            shape((count, FF), BF), shape((count, D), BF), shape((count, D), F32), shape((count, D), BF),
            shape((6, 8, D), F32), shape((8, FF), F32),
        ],
        scratch_shapes=[pltpu.VMEM((rows, FF), F32)],
        compiler_params=params(),
        cost_estimate=pl.CostEstimate(
            flops=2 * count * D * (4 * FF + 2 * D),
            bytes_accessed=count * (12 * D + 4 * FF + 4 * D) + 4 * D * FF + 2 * D * D,
            transcendentals=2 * count * FF,
        ),
        name="feed_forward",
    )(tokens, attended, cotangent, w_o, w_i, w_out, vecs, b_inner)


def outer_kernel(a_ref, b_ref, out_ref):
    out_ref[...] = dot_tn(a_ref[...], b_ref[...])


def weight_grad(left, right, rows=384, name="weight_grad"):
    count, height = left.shape
    columns = right.shape[1]
    return pl.pallas_call(
        outer_kernel,
        grid=(height // rows,),
        in_specs=[pl.BlockSpec((count, rows), lambda i: (0, i)), whole((count, columns))],
        out_specs=pl.BlockSpec((rows, columns), lambda i: (i, 0)),
        out_shape=jax.ShapeDtypeStruct((height, columns), F32),
        compiler_params=params(),
        cost_estimate=pl.CostEstimate(
            flops=2 * count * height * columns,
            bytes_accessed=2 * count * (height + columns) + 4 * height * columns,
            transcendentals=0,
        ),
        name=name,
    )(left, right)


def outer3_kernel(a_ref, b_ref, out_ref, sum_ref):
    out_ref[0] = dot_tn(a_ref[...], b_ref[0])
    sum_ref[0] = fold_rows(b_ref[0].astype(F32))


def qkv_weight_grad(tokens, grads):
    count = tokens.shape[0]
    return pl.pallas_call(
        outer3_kernel,
        grid=(3,),
        in_specs=[whole((count, D)), pl.BlockSpec((1, count, D), lambda i: (i, 0, 0))],
        out_specs=[pl.BlockSpec((1, D, D), lambda i: (i, 0, 0)), pl.BlockSpec((1, 8, D), lambda i: (i, 0, 0))],
        out_shape=[jax.ShapeDtypeStruct((3, D, D), F32), jax.ShapeDtypeStruct((3, 8, D), F32)],
        compiler_params=params(),
        cost_estimate=pl.CostEstimate(
            flops=6 * count * D * D, bytes_accessed=8 * count * D + 12 * D * D, transcendentals=0
        ),
        name="qkv_weight_grad",
    )(tokens, grads)


def tokens_kernel(gf_ref, g_ref, w_ref, out_ref):
    total = gf_ref[...]
    for part in range(3):
        total = total + dot_nt(g_ref[part], w_ref[:, part * D : (part + 1) * D])
    out_ref[...] = total.astype(BF)


def tokens_grad(grad_first, grads, w_qkv, rows=256):
    count = grad_first.shape[0]
    return pl.pallas_call(
        tokens_kernel,
        grid=(count // rows,),
        in_specs=[
            pl.BlockSpec((rows, D), lambda i: (i, 0)),
            pl.BlockSpec((3, rows, D), lambda i: (0, i, 0)),
            whole((D, 3 * D)),
        ],
        out_specs=pl.BlockSpec((rows, D), lambda i: (i, 0)),
        out_shape=jax.ShapeDtypeStruct((count, D), BF),
        compiler_params=params(),
        cost_estimate=pl.CostEstimate(
            flops=6 * count * D * D, bytes_accessed=12 * count * D + 6 * D * D, transcendentals=0
        ),
        name="tokens_grad",
    )(grad_first, grads, w_qkv)


def flip(value, axis, bit, size):
    return lax.ppermute(value, axis, [(i, i ^ (1 << bit)) for i in range(size)])


def bits_of(size):
    return size.bit_length() - 1


def reduce_rows(matrix, sizes):
    wide_bits, narrow_bits = bits_of(sizes["wide"]), bits_of(sizes["narrow"])
    index = {axis: lax.axis_index(axis) for axis in sizes}
    rows, columns = matrix.shape
    half = columns // 2
    own = rows // (sizes["wide"] * sizes["narrow"])
    side = index["narrow"] & 1
    give = lax.dynamic_slice_in_dim(matrix, (1 - side) * half, half, 1).astype(BF)
    keep = lax.dynamic_slice_in_dim(matrix, side * half, half, 1)
    total = keep + flip(give, "narrow", 0, sizes["narrow"]).astype(F32)
    slots = [("wide", b) for b in reversed(range(wide_bits))]
    slots += [("narrow", b) for b in reversed(range(1, narrow_bits))]
    total = total.reshape([2] * len(slots) + [2 * own, half])
    near = [("narrow", b) for b in range(1, narrow_bits)]
    far = [("wide", b) for b in range(1, wide_bits)]
    orders = (near + [("wide", 0)] + far, [("wide", 0)] + near + far[::-1])
    width = half // len(orders)
    done = []
    state = [(total[..., i * width : (i + 1) * width], list(slots)) for i in range(len(orders))]
    for step in range(len(slots)):
        for i, order in enumerate(orders):
            value, left = state[i]
            axis, bit = order[step]
            place = left.index((axis, bit))
            mine = (index[axis] >> bit) & 1
            give = lax.dynamic_index_in_dim(value, 1 - mine, place, keepdims=False).astype(BF)
            keep = lax.dynamic_index_in_dim(value, mine, place, keepdims=False)
            value = keep + flip(give, axis, bit, sizes[axis]).astype(F32)
            state[i] = (value, left[:place] + left[place + 1 :])
    total = jnp.concatenate([value for value, _ in state], axis=1)
    give = lax.dynamic_slice_in_dim(total, (1 - side) * own, own, 0)
    keep = lax.dynamic_slice_in_dim(total, side * own, own, 0)
    got = flip(give, "narrow", 0, sizes["narrow"])
    return jnp.where(
        side == 0, jnp.concatenate([keep, got], axis=1), jnp.concatenate([got, keep], axis=1)
    )


def pack_sums(vectors):
    block = jnp.stack(vectors, axis=1)
    return jnp.pad(block, ((0, 0), (0, -block.shape[1] % 256)))


def body(sizes, tokens, cotangent, lengths, buckets, w_query, w_key, w_value, w_output, b_query, b_value,
         b_output, gain_attn, shift_attn, w_inner, b_inner, w_outer, b_outer, gain_ffn, shift_ffn):
    devices = sizes["wide"] * sizes["narrow"]
    own = D // devices
    both = ("wide", "narrow")
    small = jnp.stack(
        [b_query, jnp.zeros_like(b_query), b_value, b_output, gain_attn, shift_attn, b_outer, gain_ffn, shift_ffn],
        axis=1,
    )
    small = jnp.concatenate([small, b_inner.reshape(own, CHUNKS)], axis=1)
    small = jnp.pad(small, ((0, 0), (0, 128 - small.shape[1])))
    outer_blocks = w_outer.reshape(CHUNKS, own, D)
    packed = jnp.concatenate(
        [w_query, w_key, w_value, w_output, w_inner] + [outer_blocks[c] for c in range(CHUNKS)] + [small], axis=1
    )
    full = lax.all_gather(packed, both, axis=0, tiled=True)
    w_qkv = full[:, : 3 * D]
    w_o = full[:, 3 * D : 4 * D]
    w_i = full[:, 4 * D : 8 * D]
    w_out = full[:, 8 * D : 12 * D].reshape(devices, own, CHUNKS, D).transpose(0, 2, 1, 3).reshape(FF, D)
    vectors = full[:, 12 * D :].astype(F32)
    vecs = vectors[:, :16].T
    bi = vectors[:, 9 : 9 + CHUNKS].reshape(1, FF)

    factor = jnp.where(buckets[0] == 0, 1, jnp.where(buckets[0] == 1, 2, 4)).astype(jnp.int32)
    limits = jnp.minimum(lengths, BLEN * factor).astype(jnp.int32)

    qkv = project_qkv(tokens, w_qkv, vecs[:8])
    attended, lse = heads_forward(qkv, limits)
    layer_out, normed_low, active, branch, hidden_grad, first_low, grad_first, attended_grad, sums, bi_sums = (
        feed_forward(tokens, attended, cotangent, w_o, w_i, w_out, vecs, bi)
    )
    outer_grad = weight_grad(active, branch, name="outer_grad")
    inner_grad = weight_grad(normed_low, hidden_grad, name="inner_grad")
    output_grad = weight_grad(attended, first_low, name="output_grad")
    sums = jnp.sum(sums, axis=1)
    bi_sums = jnp.sum(bi_sums, axis=0).reshape(D, CHUNKS)
    outer_rows = outer_grad.reshape(devices, CHUNKS, own, D).transpose(0, 2, 1, 3).reshape(D, FF)
    ffn_sums = jnp.concatenate([sums.T, bi_sums], axis=1)
    ffn_sums = jnp.pad(ffn_sums, ((0, 0), (0, 512 - ffn_sums.shape[1])))
    ffn_own = reduce_rows(jnp.concatenate([inner_grad, outer_rows, ffn_sums], axis=1), sizes)

    grads = heads_backward(qkv, attended_grad, lse, limits)
    qkv_grad, qkv_sums = qkv_weight_grad(tokens, grads)
    qkv_sums = jnp.sum(qkv_sums, axis=1).T
    qkv_sums = jnp.pad(qkv_sums, ((0, 0), (0, 512 - qkv_sums.shape[1])))
    attn_own = reduce_rows(
        jnp.concatenate([qkv_grad[0], qkv_grad[1], qkv_grad[2], output_grad, qkv_sums], axis=1), sizes
    )
    grad_tokens = tokens_grad(grad_first, grads, w_qkv)

    sums_own = ffn_own[:, 2 * FF :]
    attn_sums = attn_own[:, 4 * D :]
    return (
        layer_out,
        grad_tokens,
        attn_own[:, :D],
        attn_own[:, D : 2 * D],
        attn_own[:, 2 * D : 3 * D],
        attn_own[:, 3 * D : 4 * D],
        attn_sums[:, 0],
        attn_sums[:, 2],
        sums_own[:, 5],
        sums_own[:, 3],
        sums_own[:, 4],
        ffn_own[:, :FF],
        sums_own[:, 6 : 6 + CHUNKS].reshape(own * CHUNKS),
        ffn_own[:, FF : 2 * FF].reshape(own, CHUNKS, D).transpose(1, 0, 2).reshape(CHUNKS * own, D),
        sums_own[:, 2],
        sums_own[:, 0],
        sums_own[:, 1],
    )


def solution(mesh):
    rows, vector = P(("wide", "narrow"), None), P(("wide", "narrow"))
    sizes = {axis: mesh.shape[axis] for axis in ("wide", "narrow")}
    return jax.shard_map(
        partial(body, sizes),
        mesh=mesh,
        in_specs=(rows, rows, vector, vector) + (rows,) * 4 + (vector,) * 5
        + (rows, vector, rows, vector, vector, vector),
        out_specs=(rows,) * 6 + (vector,) * 5 + (rows, vector, rows, vector, vector, vector),
        check_vma=False,
    )
```

time: 1230 us -> 513 us (0.42)
  waiting for transfers between devices: 804 us -> 197 us
  matrix products: 147 us -> 0 us
  blocking collectives: 138 us -> 0 us
  Pallas kernels: 0 us -> 124 us
  local copies, waits for them, and re-layouts: 77.9 us -> 109 us
  loops' own time: 23.8 us -> 0 us
  other arithmetic: 17.2 us -> 39.7 us
  starting transfers between devices: 0.77 us -> 18.2 us
    reduce_scatter x3 -> x0, waiting for transfers between devices: 388 us -> none  [the longest x1 142 us: ffn_reduce(): lax.psum_scatter(outer_grad, ('wide', 'narrow'), scatter_dimension=0, til...]
    unnamed x15 -> x1, waiting for transfers between devices: 206 us -> 0.02 us
    dot_general x32 -> x0, matrix products: 147 us -> none  [the longest x6 61.9 us: product(): return jnp.dot(left_side, right_side, preferred_element_type=jnp.float32)]
    unnamed x2 -> x0, blocking collectives: 138 us -> none
    pallas_call x0 -> x9, Pallas kernels: none -> 124 us  [the longest x1 42.7 us: feed_forward(): pl.pallas_call(ffn_kernel, grid=(count // rows,), in_specs=[narrow, narro...]
    all_gather x6 -> x1, waiting for transfers between devices: 210 us -> 105 us  [body(): full = lax.all_gather(packed, both, axis=0, tiled=True)]
    ppermute x0 -> x20, waiting for transfers between devices: none -> 92.2 us  [flip(): return lax.ppermute(value, axis, [(i, i ^ 1 << bit) for i in range(size)])]
    another operation x4 -> x0, loops' own time: 23.8 us -> none  [the longest x1 13.3 us: body(): lax.switch(bucket_now, [partial(heads_forward, key_span) for key_span in...]
  transfers between devices with their start and end apart: 12 -> 21, of which waited for: 10 -> 18; matrix products, arithmetic and copies ran while one was open for 12% -> 12% of each run, Pallas kernels for 0% -> 6%
where the time goes in v1:
time: 513 us; the launch traced here: 503 us
  waiting for transfers between devices  197 us (38%)
  Pallas kernels  124 us (24%)
  local copies, waits for them, and re-layouts  109 us (21%)
  other arithmetic  39.7 us (8%)
  starting transfers between devices  18.2 us (4%)
  between operations  15.4 us (3%)
    all_gather x1, waiting for transfers between devices, body(): full = lax.all_gather(packed, both, axis=0, tiled=True)  105 us
    ppermute x20, waiting for transfers between devices, flip(): return lax.ppermute(value, axis, [(i, i ^ 1 << bit) for i in range(size)])  92.2 us
    pallas_call x1, Pallas kernels, feed_forward(): pl.pallas_call(ffn_kernel, grid=(count // rows,), in_specs=[narrow, narro...  42.7 us
    unnamed x30, local copies, waits for them, and re-layouts  32 us
    pallas_call x3, Pallas kernels, weight_grad(): pl.pallas_call(outer_kernel, grid=(height // rows,), in_specs=[pl.BlockSp...  26.8 us
    ppermute x20, starting transfers between devices, flip(): return lax.ppermute(value, axis, [(i, i ^ 1 << bit) for i in range(size)])  18.1 us
    pallas_call x1, Pallas kernels, heads_backward(): pl.pallas_call(partial(by_blocks, backward_block), grid_spec=pltpu.Prefet...  16.6 us
    concatenate x1, other arithmetic, body(): jnp.concatenate([inner_grad, outer_rows, ffn_sums], axis=1)  14.9 us
  transfers between devices with their start and end apart: 21, of which 18 were waited for; matrix products, arithmetic and copies ran while one was open for 12% of the time, Pallas kernels for 6%

profile of v1, /device:TPU:0, one launch (start us, length us, event | category | flops | bytes accessed | tf_op | source)
XLA Modules:
  0.0 503.3 jit_solution(10584290254848071826)
XLA Ops:
  23.8 105.1 %all-gather.2.cloned.1.call-done = bf16[768,9344]{1,0:T(8,128)(2,1)} async-done(((bf16[24,9344]{1,0:T(8,128)(2,1)}), bf16[768,9344]{1,0:T(8,128)(2,1)}) %all-gather.2.cloned.1.call-update) | async-done | bytes 14352400 | tf_op jit(solution)/shard_map/all_gather | solution.py:452
  131.6 8.2 %fusion.24 = (bf16[768,3072]{1,0:T(8,128)(2,1)}, bf16[768,3072]{1,0:T(8,128)(2,1)}) fusion(bf16[768,9344]{1,0:T(8,128)(2,1)} %all-gather.2.cloned.1.call-done), kind=kLoop, calls=%fused_computation.108 | loop fusion | bytes 18874368 | tf_op jit(solution)/shard_map/slice | solution.py:456
  139.7 9.8 %reshape.107 = bf16[32,24,4,768]{3,2,1,0:T(4,128)(2,1)} reshape(bf16[768,3072]{1,0:T(8,128)(2,1)} %get-tuple-element.53) | data formatting | bytes 9437184 | tf_op jit(solution)/shard_map/reshape | solution.py:456
  149.5 5.4 %copy.99 = bf16[32,4,24,768]{3,2,1,0:T(8,128)(2,1)} copy(bf16[32,4,24,768]{3,1,2,0:T(4,128)(2,1)} %bitcast.113) | data formatting | bytes 9437184 | tf_op jit(solution)/shard_map/transpose | solution.py:456
  159.9 7.9 %project_qkv.1.refs_0_ = bf16[3,1024,768]{2,1,0:T(8,128)(2,1)} custom-call(bf16[1024,768]{1,0:T(8,128)(2,1)} %a_ref.1, bf16[768,2304]{1,0:T(8,128)(2,1)} %slice.151.w_ref, f32[8,768]{1,0:T(8,128)} %copy.98.b_ref), custom_call_target="tpu_custom_call" | custom-call | flops 3623878656 | bytes 9830400 | tf_op jit(solution)/shard_map/project_qkv/pallas_call | solution.py:59
  167.8 13.1 %heads_forward.1 = (bf16[1024,768]{1,0:T(8,128)(2,1)}, f32[2,6,2,512]{3,2,1,0:T(2,128)}) custom-call(s32[2]{0:T(128)} %broadcast_minimum_fusion.limits_ref, bf16[3,1024,768]{2,1,0:T(8,128)(2,1)} %project_qkv.1.refs_0_), custom_call_target="tpu_custom_call" | custom-call | flops 6442450944 | bytes 6291456 | tf_op jit(solution)/shard_map/heads_forward/pallas_call | solution.py:150
  183.3 42.7 %feed_forward.1 = (bf16[1024,768]{1,0:T(8,128)(2,1)}, bf16[1024,768]{1,0:T(8,128)(2,1)}, bf16[1024,3072]{1,0:T(8,128)(2,1)}, bf16[1024,768]{1,0:T(8,128)(2,1)}, ...) custom-call(bf16[1024,768]{1,0:T(8,128)(2,1)} %a_ref.1, ...), custom_call_target="tpu_custom_call" | custom-call | flops 21743271936 | bytes 35782656 | tf_op jit(solution)/shard_map/feed_forward/pallas_call | solution.py:294
  226.0 16.6 %heads_backward.1.g_ref.b_ref = bf16[3,1024,768]{2,1,0:T(8,128)(2,1)} custom-call(s32[2]{0:T(128)} %broadcast_minimum_fusion.limits_ref, bf16[3,1024,768]{2,1,0:T(8,128)(2,1)} %project_qkv.1.refs_0_, bf16[1024,768]{1,0:T(8,128)(2,1)} %get-tuple-element.34.refs_1_, f32[2,6,2,512]{3,2,1,0:T(2,128)} %get-tuple-element.35.refs_2_), custom_call_target="tpu_custom_call" | custom-call | flops 16106127360 | bytes 11010048 | tf_op jit(solution)/shard_map/heads_backward/pallas_call | solution.py:178
  242.6 8.5 %qkv_weight_grad.1 = (f32[3,768,768]{2,1,0:T(8,128)}, f32[3,8,768]{2,1,0:T(8,128)}) custom-call(bf16[1024,768]{1,0:T(8,128)(2,1)} %a_ref.1, bf16[3,1024,768]{2,1,0:T(8,128)(2,1)} %heads_backward.1.g_ref.b_ref), custom_call_target="tpu_custom_call" | custom-call | flops 3623878656 | bytes 13369344 | tf_op jit(solution)/shard_map/qkv_weight_grad/pallas_call | solution.py:345
  278.0 12.0 %outer_grad.1 = f32[3072,768]{1,0:T(8,128)} custom-call(bf16[1024,3072]{1,0:T(8,128)(2,1)} %get-tuple-element.41.a_ref, bf16[1024,768]{1,0:T(8,128)(2,1)} %get-tuple-element.42.b_ref), custom_call_target="tpu_custom_call" | custom-call | flops 4831838208 | bytes 17301504 | tf_op jit(solution)/shard_map/outer_grad/pallas_call | solution.py:322
  290.0 11.1 %copy.104 = f32[32,24,4,768]{3,2,1,0:T(4,128)} copy(f32[32,24,4,768]{3,1,2,0:T(8,128)} %bitcast.114) | data formatting | bytes 18874368 | tf_op jit(solution)/shard_map/transpose | solution.py:474
  301.0 9.4 %copy.122 = f32[96,8,4,768]{3,1,2,0:T(8,128)} copy(f32[96,8,4,768]{3,2,1,0:T(4,128)} %bitcast.111) | data formatting | bytes 18874368
  310.7 10.4 %inner_grad.1 = f32[768,3072]{1,0:T(8,128)} custom-call(bf16[1024,768]{1,0:T(8,128)(2,1)} %get-tuple-element.39.a_ref, bf16[1024,3072]{1,0:T(8,128)(2,1)} %get-tuple-element.40.b_ref), custom_call_target="tpu_custom_call" | custom-call | flops 4831838208 | bytes 17301504 | tf_op jit(solution)/shard_map/inner_grad/pallas_call | solution.py:322
  321.1 14.9 %pad_maximum_fusion = f32[768,6656]{1,0:T(8,128)} fusion(f32[768,512]{1,0:T(8,128)S(1)} %select_maximum_fusion, f32[768,3072]{1,0:T(8,128)} %bitcast.110, f32[768,3072]{1,0:T(8,128)} %inner_grad.1), kind=kLoop, calls=%fused_computation | loop fusion | flops 10223616 | bytes 40894464 | tf_op jit(solution)/shard_map/concatenate | solution.py:477
  336.1 6.6 %dynamic-slice_convert_fusion = bf16[768,3328]{1,0:T(8,128)(2,1)} fusion(f32[768,6656]{1,0:T(8,128)} %pad_maximum_fusion, s32[]{:T(128)S(6)} %select_n.124), kind=kLoop, calls=%fused_computation.2 | loop fusion | bytes 10223620 | tf_op jit(solution)/shard_map/convert_element_type | solution.py:401
  354.4 14.9 %collective-permute-done.1 = bf16[2,2,2,48,896]{4,3,0,1,2:T(8,128)(2,1)S(1)} collective-permute-done((bf16[2,2,2,48,896]{4,3,0,1,2:T(8,128)(2,1)}, bf16[2,2,2,48,896]{4,3,0,1,2:T(8,128)(2,1)S(1)}, u32[]{:S(2)}, u32[]{:S(2)}) %collective-permute-start.1) | collective-permute-done | bytes 688160 | tf_op jit(solution)/shard_map/ppermute | solution.py:387
  374.0 6.4 %collective-permute-done.2 = bf16[2,2,48,896]{3,2,0,1:T(8,128)(2,1)S(1)} collective-permute-done((bf16[2,2,48,896]{3,2,0,1:T(8,128)(2,1)S(1)}, bf16[2,2,48,896]{3,2,0,1:T(8,128)(2,1)S(1)}, u32[]{:S(2)}, u32[]{:S(2)}) %collective-permute-start.2) | collective-permute-done | bytes 344096 | tf_op jit(solution)/shard_map/ppermute | solution.py:387
  398.3 10.4 %convert_add_fusion = f32[768,3328]{1,0:T(8,128)} fusion(bf16[768,3328]{1,0:T(8,128)(2,1)} %collective-permute-done.10, f32[768,6656]{1,0:T(8,128)} %pad_maximum_fusion, s32[]{:T(128)S(6)} %select_n.123), kind=kLoop, calls=%fused_computation.1 | loop fusion | flops 5111808 | bytes 25559044 | tf_op jit(solution)/shard_map/add | solution.py:403
  408.7 4.7 fusion.25
  419.5 8.5 %tokens_grad.1 = bf16[1024,768]{1,0:T(8,128)(2,1)} custom-call(f32[1024,768]{1,0:T(8,128)} %get-tuple-element.33.gf_ref, bf16[3,1024,768]{2,1,0:T(8,128)(2,1)} %heads_backward.1.g_ref.b_ref, bf16[768,2304]{1,0:T(8,128)(2,1)} %slice.151.w_ref), custom_call_target="tpu_custom_call" | custom-call | flops 3623878656 | bytes 12976128 | tf_op jit(solution)/shard_map/tokens_grad/pallas_call | solution.py:368
  429.1 11.4 %collective-permute-done.11 = bf16[2,2,2,48,1664]{4,3,0,1,2:T(8,128)(2,1)S(1)} collective-permute-done((bf16[2,2,2,48,1664]{4,3,0,1,2:T(8,128)(2,1)S(1)}, bf16[2,2,2,48,1664]{4,3,0,1,2:T(8,128)(2,1)S(1)}, u32[]{:S(2)}, u32[]{:S(2)}) %collective-permute-start.11) | collective-permute-done | bytes 1277984 | tf_op jit(solution)/shard_map/ppermute | solution.py:387
  450.1 12.0 %collective-permute-done.12 = bf16[2,2,48,1664]{3,2,0,1:T(8,128)(2,1)S(1)} collective-permute-done((bf16[2,2,48,1664]{3,2,0,1:T(8,128)(2,1)S(1)}, bf16[2,2,48,1664]{3,2,0,1:T(8,128)(2,1)S(1)}, u32[]{:S(2)}, u32[]{:S(2)}) %collective-permute-start.12) | collective-permute-done | bytes 639008 | tf_op jit(solution)/shard_map/ppermute | solution.py:387
  465.1 9.3 %collective-permute-done.13 = bf16[2,48,1664]{2,1,0:T(8,128)(2,1)S(1)} collective-permute-done((bf16[2,48,1664]{2,1,0:T(8,128)(2,1)S(1)}, bf16[2,48,1664]{2,1,0:T(8,128)(2,1)S(1)}, u32[]{:S(2)}, u32[]{:S(2)}) %collective-permute-start.13) | collective-permute-done | bytes 319520 | tf_op jit(solution)/shard_map/ppermute | solution.py:387
  475.4 10.5 %collective-permute-done.17 = bf16[2,48,1664]{2,1,0:T(8,128)(2,1)S(1)} collective-permute-done((bf16[2,48,1664]{2,1,0:T(8,128)(2,1)S(1)}, bf16[2,48,1664]{2,1,0:T(8,128)(2,1)S(1)}, u32[]{:S(2)}, u32[]{:S(2)}) %collective-permute-start.17) | collective-permute-done | bytes 319520 | tf_op jit(solution)/shard_map/ppermute | solution.py:387
  (141 shorter events, 118.1 us)
Async XLA Ops:
  7.2 121.7 %all-gather.2.cloned.1.call-start = ((), (), s32[]{:S(2)}) async-start(), calls=%async_computation | async-start | bytes 14800896 | tf_op jit(solution)/shard_map/all_gather | solution.py:452
  270.2 7.1 %copy-start.6 = (f32[8,3072]{1,0:T(8,128)S(1)}, f32[8,3072]{1,0:T(8,128)}, u32[]{:S(2)}) copy-start(f32[8,3072]{1,0:T(8,128)} %get-tuple-element.44) | copy-start | bytes 294916
  270.2 7.5 %copy-start.5 = (f32[6,8,768]{2,1,0:T(8,128)S(1)}, f32[6,8,768]{2,1,0:T(8,128)}, u32[]{:S(2)}) copy-start(f32[6,8,768]{2,1,0:T(8,128)} %get-tuple-element.43) | copy-start | bytes 442372
  274.7 68.1 %collective-permute-start = (bf16[768,1792]{1,0:T(8,128)(2,1)}, bf16[768,1792]{1,0:T(8,128)(2,1)}, u32[]{:S(2)}, u32[]{:S(2)}) collective-permute-start(bf16[768,1792]{1,0:T(8,128)(2,1)} %dynamic-slice_convert_fusion.1), channel_id=1, source_target_pairs={{0,1},{1,0},{2,3},{3,2},{4,5},{5,4},{6,7},{7,6},{8,9},{9,8},{10,11... | collective-permute-start | bytes 8257544 | tf_op jit(solution)/shard_map/ppermute | solution.py:387
  342.7 55.6 %collective-permute-start.10 = (bf16[768,3328]{1,0:T(8,128)(2,1)}, bf16[768,3328]{1,0:T(8,128)(2,1)}, u32[]{:S(2)}, u32[]{:S(2)}) collective-permute-start(bf16[768,3328]{1,0:T(8,128)(2,1)} %dynamic-slice_convert_fusion), channel_id=1, source_target_pairs={{0,1},{1,0},{2,3},{3,2},{4,5},{5,4},{6,7},{7,6},{8,9},{9,8},{10,11... | collective-permute-start | bytes 15335432 | tf_op jit(solution)/shard_map/ppermute | solution.py:387
  349.5 19.7 %collective-permute-start.1 = (bf16[2,2,2,48,896]{4,3,0,1,2:T(8,128)(2,1)}, bf16[2,2,2,48,896]{4,3,0,1,2:T(8,128)(2,1)S(1)}, u32[]{:S(2)}, u32[]{:S(2)}) collective-permute-start(bf16[2,2,2,48,896]{4,3,0,1,2:T(8,128)(2,1)} %fusion.6), channel_id=1, source_target_pairs={{0,2},{1,3},{2,0},{3,1},{4,6},{5,7},{6,4},{7,5},{8,10},{9,11},{10,... | collective-permute-start | bytes 2064392 | tf_op jit(solution)/shard_map/ppermute | solution.py:387
  354.4 17.4 %collective-permute-start.5 = (bf16[2,2,2,48,896]{4,3,1,0,2:T(8,128)(2,1)}, bf16[2,2,2,48,896]{4,3,1,0,2:T(8,128)(2,1)}, u32[]{:S(2)}, u32[]{:S(2)}) collective-permute-start(bf16[2,2,2,48,896]{4,3,1,0,2:T(8,128)(2,1)} %fusion.7), channel_id=1, source_target_pairs={{0,4},{4,0},{8,12},{12,8},{16,20},{20,16},{24,28},{28,24},{1,5},{5... | collective-permute-start | bytes 2064392 | tf_op jit(solution)/shard_map/ppermute | solution.py:387
  370.8 9.6 %collective-permute-start.2 = (bf16[2,2,48,896]{3,2,0,1:T(8,128)(2,1)S(1)}, bf16[2,2,48,896]{3,2,0,1:T(8,128)(2,1)S(1)}, u32[]{:S(2)}, u32[]{:S(2)}) collective-permute-start(bf16[2,2,48,896]{3,2,0,1:T(8,128)(2,1)S(1)} %fusion.10), channel_id=1, source_target_pairs={{0,4},{4,0},{8,12},{12,8},{16,20},{20,16},{24,28},{28,24},{1,5},{5... | collective-permute-start | bytes 1032200 | tf_op jit(solution)/shard_map/ppermute | solution.py:387
  373.1 8.9 %collective-permute-start.6 = (bf16[2,2,48,896]{3,2,1,0:T(8,128)(2,1)S(1)}, bf16[2,2,48,896]{3,2,1,0:T(8,128)(2,1)S(1)}, u32[]{:S(2)}, u32[]{:S(2)}) collective-permute-start(bf16[2,2,48,896]{3,2,1,0:T(8,128)(2,1)S(1)} %fusion.11), channel_id=1, source_target_pairs={{0,2},{1,3},{2,0},{3,1},{4,6},{5,7},{6,4},{7,5},{8,10},{9,11},{10,... | collective-permute-start | bytes 1032200 | tf_op jit(solution)/shard_map/ppermute | solution.py:387
  380.5 7.5 %collective-permute-start.3 = (bf16[2,48,896]{2,1,0:T(8,128)(2,1)S(1)}, bf16[2,48,896]{2,1,0:T(8,128)(2,1)S(1)}, u32[]{:S(2)}, u32[]{:S(2)}) collective-permute-start(bf16[2,48,896]{2,1,0:T(8,128)(2,1)S(1)} %fusion.16), channel_id=1, source_target_pairs={{0,8},{4,12},{8,0},{12,4},{16,24},{20,28},{24,16},{28,20},{1,9},{5... | collective-permute-start | bytes 516104 | tf_op jit(solution)/shard_map/ppermute | solution.py:387
  382.0 11.7 %collective-permute-start.7 = (bf16[2,48,896]{2,1,0:T(8,128)(2,1)S(1)}, bf16[2,48,896]{2,1,0:T(8,128)(2,1)S(1)}, u32[]{:S(2)}, u32[]{:S(2)}) collective-permute-start(bf16[2,48,896]{2,1,0:T(8,128)(2,1)S(1)} %fusion.17), channel_id=1, source_target_pairs={{0,16},{4,20},{8,24},{12,28},{16,0},{20,4},{24,8},{28,12},{1,17},{... | collective-permute-start | bytes 516104 | tf_op jit(solution)/shard_map/ppermute | solution.py:387
  388.0 6.6 %collective-permute-start.4 = (bf16[48,896]{1,0:T(8,128)(2,1)S(1)}, bf16[48,896]{1,0:T(8,128)(2,1)S(1)}, u32[]{:S(2)}, u32[]{:S(2)}) collective-permute-start(bf16[48,896]{1,0:T(8,128)(2,1)S(1)} %fusion.22), channel_id=1, source_target_pairs={{0,16},{4,20},{8,24},{12,28},{16,0},{20,4},{24,8},{28,12},{1,17},{... | collective-permute-start | bytes 258056 | tf_op jit(solution)/shard_map/ppermute | solution.py:387
  393.7 4.6 collective-permute-start.8
  413.6 26.9 %collective-permute-start.11 = (bf16[2,2,2,48,1664]{4,3,0,1,2:T(8,128)(2,1)S(1)}, bf16[2,2,2,48,1664]{4,3,0,1,2:T(8,128)(2,1)S(1)}, u32[]{:S(2)}, u32[]{:S(2)}) collective-permute-start(bf16[2,2,2,48,1664]{4,3,0,1,2:T(8,128)(2,1)S(1)} %fusion.4), channel_id=1, source_target_pairs={{0,2},{1,3},{2,0},{3,1},{4,6},{5,7},{6,4},{7,5},{8,10},{9,11},{10,... | collective-permute-start | bytes 3833864 | tf_op jit(solution)/shard_map/ppermute | solution.py:387
  416.6 11.5 %collective-permute-start.9 = (f32[24,1792]{1,0:T(8,128)}, f32[24,1792]{1,0:T(8,128)}, u32[]{:S(2)}, u32[]{:S(2)}) collective-permute-start(f32[24,1792]{1,0:T(8,128)} %get-tuple-element.68), channel_id=1, source_target_pairs={{0,1},{1,0},{2,3},{3,2},{4,5},{5,4},{6,7},{7,6},{8,9},{9,8},{10,11... | collective-permute-start | bytes 516104 | tf_op jit(solution)/shard_map/ppermute | solution.py:387
  417.8 31.1 %collective-permute-start.15 = (bf16[2,2,2,48,1664]{4,3,1,0,2:T(8,128)(2,1)}, bf16[2,2,2,48,1664]{4,3,1,0,2:T(8,128)(2,1)S(1)}, u32[]{:S(2)}, u32[]{:S(2)}) collective-permute-start(bf16[2,2,2,48,1664]{4,3,1,0,2:T(8,128)(2,1)} %fusion.5), channel_id=1, source_target_pairs={{0,4},{4,0},{8,12},{12,8},{16,20},{20,16},{24,28},{28,24},{1,5},{5... | collective-permute-start | bytes 3833864 | tf_op jit(solution)/shard_map/ppermute | solution.py:387
  429.1 19.8 %copy-start.1 = (f32[2,2,2,2,48,1664]{5,4,3,2,1,0:T(8,128)S(1)}, f32[2,2,2,2,48,1664]{5,4,3,2,1,0:T(8,128)}, u32[]{:S(2)}) copy-start(f32[2,2,2,2,48,1664]{5,4,3,2,1,0:T(8,128)} %copy-done) | copy-start | bytes 15335428
  442.6 19.6 %collective-permute-start.12 = (bf16[2,2,48,1664]{3,2,0,1:T(8,128)(2,1)S(1)}, bf16[2,2,48,1664]{3,2,0,1:T(8,128)(2,1)S(1)}, u32[]{:S(2)}, u32[]{:S(2)}) collective-permute-start(bf16[2,2,48,1664]{3,2,0,1:T(8,128)(2,1)S(1)} %fusion.8), channel_id=1, source_target_pairs={{0,4},{4,0},{8,12},{12,8},{16,20},{20,16},{24,28},{28,24},{1,5},{5... | collective-permute-start | bytes 1916936 | tf_op jit(solution)/shard_map/ppermute | solution.py:387
  449.2 15.7 %collective-permute-start.16 = (bf16[2,2,48,1664]{3,2,1,0:T(8,128)(2,1)S(1)}, bf16[2,2,48,1664]{3,2,1,0:T(8,128)(2,1)S(1)}, u32[]{:S(2)}, u32[]{:S(2)}) collective-permute-start(bf16[2,2,48,1664]{3,2,1,0:T(8,128)(2,1)S(1)} %fusion.9), channel_id=1, source_target_pairs={{0,2},{1,3},{2,0},{3,1},{4,6},{5,7},{6,4},{7,5},{8,10},{9,11},{10,... | collective-permute-start | bytes 1916936 | tf_op jit(solution)/shard_map/ppermute | solution.py:387
  462.3 12.1 %collective-permute-start.13 = (bf16[2,48,1664]{2,1,0:T(8,128)(2,1)S(1)}, bf16[2,48,1664]{2,1,0:T(8,128)(2,1)S(1)}, u32[]{:S(2)}, u32[]{:S(2)}) collective-permute-start(bf16[2,48,1664]{2,1,0:T(8,128)(2,1)S(1)} %fusion.12), channel_id=1, source_target_pairs={{0,8},{4,12},{8,0},{12,4},{16,24},{20,28},{24,16},{28,20},{1,9},{5... | collective-permute-start | bytes 958472 | tf_op jit(solution)/shard_map/ppermute | solution.py:387
  465.1 20.9 %collective-permute-start.17 = (bf16[2,48,1664]{2,1,0:T(8,128)(2,1)S(1)}, bf16[2,48,1664]{2,1,0:T(8,128)(2,1)S(1)}, u32[]{:S(2)}, u32[]{:S(2)}) collective-permute-start(bf16[2,48,1664]{2,1,0:T(8,128)(2,1)S(1)} %fusion.13), channel_id=1, source_target_pairs={{0,16},{4,20},{8,24},{12,28},{16,0},{20,4},{24,8},{28,12},{1,17},{... | collective-permute-start | bytes 958472 | tf_op jit(solution)/shard_map/ppermute | solution.py:387
  474.5 13.2 %collective-permute-start.14 = (bf16[48,1664]{1,0:T(8,128)(2,1)S(1)}, bf16[48,1664]{1,0:T(8,128)(2,1)S(1)}, u32[]{:S(2)}, u32[]{:S(2)}) collective-permute-start(bf16[48,1664]{1,0:T(8,128)(2,1)S(1)} %fusion.20), channel_id=1, source_target_pairs={{0,16},{4,20},{8,24},{12,28},{16,0},{20,4},{24,8},{28,12},{1,17},{... | collective-permute-start | bytes 479240 | tf_op jit(solution)/shard_map/ppermute | solution.py:387
  486.1 5.3 %collective-permute-start.18 = (bf16[48,1664]{1,0:T(8,128)(2,1)S(1)}, bf16[48,1664]{1,0:T(8,128)(2,1)S(1)}, u32[]{:S(2)}, u32[]{:S(2)}) collective-permute-start(bf16[48,1664]{1,0:T(8,128)(2,1)S(1)} %fusion.21), channel_id=1, source_target_pairs={{0,8},{4,12},{8,0},{12,4},{16,24},{20,28},{24,16},{28,20},{1,9},{5... | collective-permute-start | bytes 479240 | tf_op jit(solution)/shard_map/ppermute | solution.py:387
  491.5 1.7 collective-permute-start.19
  (5 other events, 17.2 us)
Sparse Core Ops, SparseCore 0:
  22.1 106.7 all-gather.1

commit v2 on v1

--- a/solution.py
+++ b/solution.py
@@ -47,6 +47,10 @@
     return pl.BlockSpec(shape, lambda *_: (0,) * len(shape), pipeline_mode=pl.Buffered(1))
 
 
+def columns_of(block, width):
+    return pl.BlockSpec((D, width), lambda *_: (0, block), pipeline_mode=pl.Buffered(1))
+
+
 def qkv_kernel(x_ref, w_ref, b_ref, out_ref):
     x = x_ref[...]
     for part in range(3):
@@ -62,7 +66,7 @@
         in_specs=[
             pl.BlockSpec((rows, D), lambda i: (i, 0)),
             whole((D, 3 * D)),
-            whole((8, D)),
+            whole((16, D)),
         ],
         out_specs=pl.BlockSpec((3, rows, D), lambda i: (0, i, 0)),
         out_shape=jax.ShapeDtypeStruct((3, count, D), BF),
@@ -231,11 +235,11 @@
     return jnp.sum(matrix.reshape(rows // 8, 8, columns), axis=0)
 
 
-BIAS_ROWS = ("b_query", "zero", "b_value", "b_output", "gain_attn", "shift_attn", "b_outer", "gain_ffn", "shift_ffn")
+BIAS_ROWS = ("b_query", "zero", "b_value", "b_output", "gain_attn", "shift_attn", "b_outer", "gain_ffn", "shift_ffn", "b_inner")
 
 
 def ffn_kernel(
-    tok_ref, att_ref, cot_ref, wo_ref, wi_ref, wout_ref, vec_ref, bi_ref,
+    tok_ref, att_ref, cot_ref, wi_ref, wout_ref, wo_ref, vec_ref,
     out_ref, nl_ref, act_ref, bg_ref, hg_ref, fl_ref, gf_ref, ag_ref, sums_ref, bisum_ref,
     slope_ref,
 ):
@@ -254,12 +258,12 @@
     second = normed + vec("b_outer")
     for c in range(CHUNKS):
         cols = slice(c * D, (c + 1) * D)
-        hidden = dot_nn(nl, wi_ref[:, cols]) + bi_ref[:, cols]
+        hidden = dot_nn(nl, wi_ref[:, cols]) + vec_ref[BIAS_ROWS.index("b_inner") + c : BIAS_ROWS.index("b_inner") + c + 1, :]
         phi, power = normal_parts(hidden)
         active = (hidden * phi).astype(BF)
         slope_ref[:, cols] = phi + hidden * power * DENSITY
         act_ref[:, cols] = active
-        second = second + dot_nn(active, wout_ref[cols, :])
+        second = second + dot_nn(active, wout_ref[:, cols])
     unit_two, scale_two = norm_rows(second)
     out_ref[...] = (unit_two * vec("gain_ffn") + vec("shift_ffn")).astype(BF)
     cot = cot_ref[...].astype(F32)
@@ -272,7 +276,7 @@
     grad_normed = grad_second
     for c in range(CHUNKS):
         cols = slice(c * D, (c + 1) * D)
-        hg = (dot_nt(bg, wout_ref[cols, :]) * slope_ref[:, cols]).astype(BF)
+        hg = (dot_nt(bg, wout_ref[:, cols]) * slope_ref[:, cols]).astype(BF)
         hg_ref[:, cols] = hg
         bisum_ref[:, cols] += fold_rows(hg.astype(F32))
         grad_normed = grad_normed + dot_nt(hg, wi_ref[:, cols])
@@ -286,7 +290,7 @@
     ag_ref[...] = dot_nt(fl, wo_ref[...]).astype(BF)
 
 
-def feed_forward(tokens, attended, cotangent, w_o, w_i, w_out, vecs, b_inner, rows=256):
+def feed_forward(tokens, attended, cotangent, weights, vecs, rows=256):
     count = tokens.shape[0]
     narrow = pl.BlockSpec((rows, D), lambda i: (i, 0))
     wide = pl.BlockSpec((rows, FF), lambda i: (i, 0))
@@ -294,7 +298,11 @@
     return pl.pallas_call(
         ffn_kernel,
         grid=(count // rows,),
-        in_specs=[narrow, narrow, narrow, whole((D, D)), whole((D, FF)), whole((FF, D)), whole((16, D)), whole((1, FF))],
+        in_specs=[
+            narrow, narrow, narrow,
+            columns_of(0, FF), columns_of(1, FF), columns_of(2 * CHUNKS, D),
+            whole((16, D)),
+        ],
         out_specs=[narrow, narrow, wide, narrow, wide, narrow, narrow, narrow, whole((6, 8, D)), whole((8, FF))],
         out_shape=[
             shape((count, D), BF), shape((count, D), BF), shape((count, FF), BF), shape((count, D), BF),
@@ -309,51 +317,89 @@
             transcendentals=2 * count * FF,
         ),
         name="feed_forward",
-    )(tokens, attended, cotangent, w_o, w_i, w_out, vecs, b_inner)
+    )(tokens, attended, cotangent, weights, weights, weights, vecs)
 
 
 def outer_kernel(a_ref, b_ref, out_ref):
-    out_ref[...] = dot_tn(a_ref[...], b_ref[...])
-
-
-def weight_grad(left, right, rows=384, name="weight_grad"):
-    count, height = left.shape
-    columns = right.shape[1]
+    out_ref[...] = dot_tn(a_ref[...], b_ref[...]).astype(BF)
+
+
+def outer_weight_grad(active, branch, rows=384):
+    count = active.shape[0]
+    split = D // rows
     return pl.pallas_call(
         outer_kernel,
-        grid=(height // rows,),
-        in_specs=[pl.BlockSpec((count, rows), lambda i: (0, i)), whole((count, columns))],
-        out_specs=pl.BlockSpec((rows, columns), lambda i: (i, 0)),
-        out_shape=jax.ShapeDtypeStruct((height, columns), F32),
-        compiler_params=params(),
-        cost_estimate=pl.CostEstimate(
-            flops=2 * count * height * columns,
-            bytes_accessed=2 * count * (height + columns) + 4 * height * columns,
-            transcendentals=0,
-        ),
-        name=name,
-    )(left, right)
-
-
-def outer3_kernel(a_ref, b_ref, out_ref, sum_ref):
-    out_ref[0] = dot_tn(a_ref[...], b_ref[0])
-    sum_ref[0] = fold_rows(b_ref[0].astype(F32))
-
-
-def qkv_weight_grad(tokens, grads):
+        grid=(CHUNKS, split),
+        in_specs=[pl.BlockSpec((count, rows), lambda c, m: (0, c * split + m)), whole((count, D))],
+        out_specs=pl.BlockSpec((rows, D), lambda c, m: (m, c)),
+        out_shape=jax.ShapeDtypeStruct((D, FF), BF),
+        compiler_params=params(),
+        cost_estimate=pl.CostEstimate(
+            flops=2 * count * FF * D, bytes_accessed=2 * count * (FF + D) + 2 * FF * D, transcendentals=0
+        ),
+        name="outer_weight_grad",
+    )(active, branch)
+
+
+def inner_kernel(a_ref, b_ref, out_ref, turned_ref):
+    @pl.when(pl.program_id(0) == 0)
+    def _():
+        turned_ref[...] = a_ref[...].T
+
+    out_ref[...] = dot_nn(turned_ref[...], b_ref[...])
+
+
+def inner_weight_grad(normed, hidden_grad, columns=768):
+    count = normed.shape[0]
+    return pl.pallas_call(
+        inner_kernel,
+        grid=(FF // columns,),
+        in_specs=[whole((count, D)), pl.BlockSpec((count, columns), lambda i: (0, i))],
+        out_specs=pl.BlockSpec((D, columns), lambda i: (0, i)),
+        out_shape=jax.ShapeDtypeStruct((D, FF), F32),
+        scratch_shapes=[pltpu.VMEM((D, count), BF)],
+        compiler_params=params(),
+        cost_estimate=pl.CostEstimate(
+            flops=2 * count * FF * D, bytes_accessed=2 * count * (FF + D) + 4 * FF * D, transcendentals=0
+        ),
+        name="inner_weight_grad",
+    )(normed, hidden_grad)
+
+
+SUMS = 128
+
+
+def attn_weights_kernel(tok_ref, att_ref, g_ref, gcols_ref, fl_ref, sums_ref, out_ref):
+    count = tok_ref.shape[0]
+    turned = tok_ref[...].T
+    for part in range(3):
+        out_ref[:, part * D : (part + 1) * D] = dot_nn(turned, g_ref[part])
+    out_ref[:, 3 * D : 4 * D] = dot_tn(att_ref[...], fl_ref[...])
+    place = lax.broadcasted_iota(jnp.int32, (count, SUMS), 1)
+    sums = sums_ref[...]
+    for part, column in ((0, 10), (2, 11)):
+        sums = sums + dot_tn(gcols_ref[part], (place == column).astype(BF))
+    out_ref[:, 4 * D :] = sums
+
+
+def attn_weight_grads(tokens, attended, grads, first_low, sums, rows=384):
     count = tokens.shape[0]
-    return pl.pallas_call(
-        outer3_kernel,
-        grid=(3,),
-        in_specs=[whole((count, D)), pl.BlockSpec((1, count, D), lambda i: (i, 0, 0))],
-        out_specs=[pl.BlockSpec((1, D, D), lambda i: (i, 0, 0)), pl.BlockSpec((1, 8, D), lambda i: (i, 0, 0))],
-        out_shape=[jax.ShapeDtypeStruct((3, D, D), F32), jax.ShapeDtypeStruct((3, 8, D), F32)],
-        compiler_params=params(),
-        cost_estimate=pl.CostEstimate(
-            flops=6 * count * D * D, bytes_accessed=8 * count * D + 12 * D * D, transcendentals=0
-        ),
-        name="qkv_weight_grad",
-    )(tokens, grads)
+    narrow = pl.BlockSpec((count, rows), lambda i: (0, i))
+    return pl.pallas_call(
+        attn_weights_kernel,
+        grid=(D // rows,),
+        in_specs=[
+            narrow, narrow, whole((3, count, D)), pl.BlockSpec((3, count, rows), lambda i: (0, 0, i)),
+            whole((count, D)), pl.BlockSpec((rows, SUMS), lambda i: (i, 0)),
+        ],
+        out_specs=pl.BlockSpec((rows, 4 * D + SUMS), lambda i: (i, 0)),
+        out_shape=jax.ShapeDtypeStruct((D, 4 * D + SUMS), F32),
+        compiler_params=params(),
+        cost_estimate=pl.CostEstimate(
+            flops=8 * count * D * D, bytes_accessed=18 * count * D + 16 * D * D, transcendentals=0
+        ),
+        name="attn_weight_grads",
+    )(tokens, attended, grads, grads, first_low, sums)
 
 
 def tokens_kernel(gf_ref, g_ref, w_ref, out_ref):
@@ -383,110 +429,82 @@
     )(grad_first, grads, w_qkv)
 
 
-def flip(value, axis, bit, size):
-    return lax.ppermute(value, axis, [(i, i ^ (1 << bit)) for i in range(size)])
-
-
-def bits_of(size):
-    return size.bit_length() - 1
-
-
-def reduce_rows(matrix, sizes):
-    wide_bits, narrow_bits = bits_of(sizes["wide"]), bits_of(sizes["narrow"])
-    index = {axis: lax.axis_index(axis) for axis in sizes}
+AXES = ("hi", "lo", "far", "near")
+CHIPS = AXES[:3]
+
+
+def swap_near(value):
+    return lax.ppermute(value, "near", [(0, 1), (1, 0)])
+
+
+def exchange(value):
+    return lax.all_to_all(value, CHIPS, 0, 0, tiled=True)
+
+
+def gather_rows(block, sizes):
+    own, columns = block.shape
+    chips = sizes["hi"] * sizes["lo"] * sizes["far"]
+    mine = exchange(jnp.broadcast_to(block[None], (chips, own, columns)))
+    other = swap_near(mine)
+    place = lax.broadcasted_iota(jnp.int32, (chips, 2, own, columns), 1)
+    full = jnp.where(place == lax.axis_index("near"), mine[:, None], other[:, None])
+    return lax.optimization_barrier(full).reshape(chips * 2 * own, columns)
+
+
+def scatter_rows(matrix, sizes):
     rows, columns = matrix.shape
-    half = columns // 2
-    own = rows // (sizes["wide"] * sizes["narrow"])
-    side = index["narrow"] & 1
-    give = lax.dynamic_slice_in_dim(matrix, (1 - side) * half, half, 1).astype(BF)
-    keep = lax.dynamic_slice_in_dim(matrix, side * half, half, 1)
-    total = keep + flip(give, "narrow", 0, sizes["narrow"]).astype(F32)
-    slots = [("wide", b) for b in reversed(range(wide_bits))]
-    slots += [("narrow", b) for b in reversed(range(1, narrow_bits))]
-    total = total.reshape([2] * len(slots) + [2 * own, half])
-    near = [("narrow", b) for b in range(1, narrow_bits)]
-    far = [("wide", b) for b in range(1, wide_bits)]
-    orders = (near + [("wide", 0)] + far, [("wide", 0)] + near + far[::-1])
-    width = half // len(orders)
-    done = []
-    state = [(total[..., i * width : (i + 1) * width], list(slots)) for i in range(len(orders))]
-    for step in range(len(slots)):
-        for i, order in enumerate(orders):
-            value, left = state[i]
-            axis, bit = order[step]
-            place = left.index((axis, bit))
-            mine = (index[axis] >> bit) & 1
-            give = lax.dynamic_index_in_dim(value, 1 - mine, place, keepdims=False).astype(BF)
-            keep = lax.dynamic_index_in_dim(value, mine, place, keepdims=False)
-            value = keep + flip(give, axis, bit, sizes[axis]).astype(F32)
-            state[i] = (value, left[:place] + left[place + 1 :])
-    total = jnp.concatenate([value for value, _ in state], axis=1)
-    give = lax.dynamic_slice_in_dim(total, (1 - side) * own, own, 0)
-    keep = lax.dynamic_slice_in_dim(total, side * own, own, 0)
-    got = flip(give, "narrow", 0, sizes["narrow"])
-    return jnp.where(
-        side == 0, jnp.concatenate([keep, got], axis=1), jnp.concatenate([got, keep], axis=1)
-    )
-
-
-def pack_sums(vectors):
-    block = jnp.stack(vectors, axis=1)
-    return jnp.pad(block, ((0, 0), (0, -block.shape[1] % 256)))
+    chips = sizes["hi"] * sizes["lo"] * sizes["far"]
+    own = rows // (2 * chips)
+    side = lax.axis_index("near")
+    parts = matrix.reshape(chips, 2, own, columns)
+    give = lax.dynamic_index_in_dim(parts, 1 - side, 1, keepdims=False).astype(BF)
+    keep = lax.dynamic_index_in_dim(parts, side, 1, keepdims=False)
+    pair = (keep + swap_near(give).astype(F32)).astype(BF)
+    return pair, lambda: jnp.sum(exchange(pair).astype(F32), axis=0)
 
 
 def body(sizes, tokens, cotangent, lengths, buckets, w_query, w_key, w_value, w_output, b_query, b_value,
          b_output, gain_attn, shift_attn, w_inner, b_inner, w_outer, b_outer, gain_ffn, shift_ffn):
-    devices = sizes["wide"] * sizes["narrow"]
-    own = D // devices
-    both = ("wide", "narrow")
+    own = w_query.shape[0]
+    devices = D // own
+    inner_turned = w_inner.reshape(own, devices, CHUNKS, own).transpose(0, 2, 1, 3).reshape(own, FF)
+    outer_blocks = w_outer.reshape(CHUNKS, own, D)
+    ffn_pack = jnp.concatenate([inner_turned] + [outer_blocks[c] for c in range(CHUNKS)] + [w_output], axis=1)
+    ffn_weights = lax.all_gather(ffn_pack, AXES, axis=0, tiled=True)
+
     small = jnp.stack(
         [b_query, jnp.zeros_like(b_query), b_value, b_output, gain_attn, shift_attn, b_outer, gain_ffn, shift_ffn],
         axis=1,
     )
-    small = jnp.concatenate([small, b_inner.reshape(own, CHUNKS)], axis=1)
+    small = jnp.concatenate([small, b_inner.reshape(CHUNKS, own).T], axis=1)
     small = jnp.pad(small, ((0, 0), (0, 128 - small.shape[1])))
-    outer_blocks = w_outer.reshape(CHUNKS, own, D)
-    packed = jnp.concatenate(
-        [w_query, w_key, w_value, w_output, w_inner] + [outer_blocks[c] for c in range(CHUNKS)] + [small], axis=1
-    )
-    full = lax.all_gather(packed, both, axis=0, tiled=True)
-    w_qkv = full[:, : 3 * D]
-    w_o = full[:, 3 * D : 4 * D]
-    w_i = full[:, 4 * D : 8 * D]
-    w_out = full[:, 8 * D : 12 * D].reshape(devices, own, CHUNKS, D).transpose(0, 2, 1, 3).reshape(FF, D)
-    vectors = full[:, 12 * D :].astype(F32)
-    vecs = vectors[:, :16].T
-    bi = vectors[:, 9 : 9 + CHUNKS].reshape(1, FF)
+    attn_weights = gather_rows(jnp.concatenate([w_query, w_key, w_value, small], axis=1), sizes)
+    vecs = attn_weights[:, 3 * D : 3 * D + 16].astype(F32).T
 
     factor = jnp.where(buckets[0] == 0, 1, jnp.where(buckets[0] == 1, 2, 4)).astype(jnp.int32)
     limits = jnp.minimum(lengths, BLEN * factor).astype(jnp.int32)
 
-    qkv = project_qkv(tokens, w_qkv, vecs[:8])
+    qkv = project_qkv(tokens, attn_weights, vecs)
     attended, lse = heads_forward(qkv, limits)
     layer_out, normed_low, active, branch, hidden_grad, first_low, grad_first, attended_grad, sums, bi_sums = (
-        feed_forward(tokens, attended, cotangent, w_o, w_i, w_out, vecs, bi)
+        feed_forward(tokens, attended, cotangent, ffn_weights, vecs)
     )
-    outer_grad = weight_grad(active, branch, name="outer_grad")
-    inner_grad = weight_grad(normed_low, hidden_grad, name="inner_grad")
-    output_grad = weight_grad(attended, first_low, name="output_grad")
-    sums = jnp.sum(sums, axis=1)
-    bi_sums = jnp.sum(bi_sums, axis=0).reshape(D, CHUNKS)
-    outer_rows = outer_grad.reshape(devices, CHUNKS, own, D).transpose(0, 2, 1, 3).reshape(D, FF)
-    ffn_sums = jnp.concatenate([sums.T, bi_sums], axis=1)
-    ffn_sums = jnp.pad(ffn_sums, ((0, 0), (0, 512 - ffn_sums.shape[1])))
-    ffn_own = reduce_rows(jnp.concatenate([inner_grad, outer_rows, ffn_sums], axis=1), sizes)
-
+    outer_grad = outer_weight_grad(active, branch)
+    outer_own = lax.psum_scatter(outer_grad, AXES, scatter_dimension=0, tiled=True)
+    normed_low, _ = lax.optimization_barrier((normed_low, outer_grad))
+    inner_grad = inner_weight_grad(normed_low, hidden_grad)
+    inner_pair, inner_finish = scatter_rows(inner_grad, sizes)
+    sums = jnp.concatenate([jnp.sum(sums, axis=1), jnp.sum(bi_sums, axis=0).reshape(CHUNKS, D)], axis=0)
+    sums = jnp.pad(sums, ((0, SUMS - sums.shape[0]), (0, 0))).T
+
+    attended_grad, _ = lax.optimization_barrier((attended_grad, inner_pair))
     grads = heads_backward(qkv, attended_grad, lse, limits)
-    qkv_grad, qkv_sums = qkv_weight_grad(tokens, grads)
-    qkv_sums = jnp.sum(qkv_sums, axis=1).T
-    qkv_sums = jnp.pad(qkv_sums, ((0, 0), (0, 512 - qkv_sums.shape[1])))
-    attn_own = reduce_rows(
-        jnp.concatenate([qkv_grad[0], qkv_grad[1], qkv_grad[2], output_grad, qkv_sums], axis=1), sizes
-    )
-    grad_tokens = tokens_grad(grad_first, grads, w_qkv)
-
-    sums_own = ffn_own[:, 2 * FF :]
-    attn_sums = attn_own[:, 4 * D :]
+    _, attn_finish = scatter_rows(attn_weight_grads(tokens, attended, grads, first_low, sums), sizes)
+    grad_tokens = tokens_grad(grad_first, grads, attn_weights)
+    inner_own = inner_finish()
+    attn_own = attn_finish()
+
+    sums_own = attn_own[:, 4 * D :]
     return (
         layer_out,
         grad_tokens,
@@ -494,14 +512,14 @@
         attn_own[:, D : 2 * D],
         attn_own[:, 2 * D : 3 * D],
         attn_own[:, 3 * D : 4 * D],
-        attn_sums[:, 0],
-        attn_sums[:, 2],
+        sums_own[:, 10],
+        sums_own[:, 11],
         sums_own[:, 5],
         sums_own[:, 3],
         sums_own[:, 4],
-        ffn_own[:, :FF],
-        sums_own[:, 6 : 6 + CHUNKS].reshape(own * CHUNKS),
-        ffn_own[:, FF : 2 * FF].reshape(own, CHUNKS, D).transpose(1, 0, 2).reshape(CHUNKS * own, D),
+        inner_own.reshape(own, CHUNKS, devices, own).transpose(0, 2, 1, 3).reshape(own, FF),
+        sums_own[:, 6 : 6 + CHUNKS].T.reshape(CHUNKS * own),
+        outer_own.astype(F32).reshape(own, CHUNKS, D).transpose(1, 0, 2).reshape(CHUNKS * own, D),
         sums_own[:, 2],
         sums_own[:, 0],
         sums_own[:, 1],
@@ -509,11 +527,13 @@
 
 
 def solution(mesh):
-    rows, vector = P(("wide", "narrow"), None), P(("wide", "narrow"))
-    sizes = {axis: mesh.shape[axis] for axis in ("wide", "narrow")}
+    wide, narrow = mesh.shape["wide"], mesh.shape["narrow"]
+    sizes = {"hi": wide // 2, "lo": 2, "far": narrow // 2, "near": 2}
+    split = jax.sharding.Mesh(mesh.devices.reshape([sizes[axis] for axis in AXES]), AXES)
+    rows, vector = P(AXES, None), P(AXES)
     return jax.shard_map(
         partial(body, sizes),
-        mesh=mesh,
+        mesh=split,
         in_specs=(rows, rows, vector, vector) + (rows,) * 4 + (vector,) * 5
         + (rows, vector, rows, vector, vector, vector),
         out_specs=(rows,) * 6 + (vector,) * 5 + (rows, vector, rows, vector, vector, vector),

time: 513 us -> 386 us (0.75); the launches traced: 503 us -> 385 us
  waiting for transfers between devices: 197 us -> 107 us
  local copies, waits for them, and re-layouts: 109 us -> 30.8 us
  blocking collectives: 0 us -> 73.8 us
  other arithmetic: 39.7 us -> 15.8 us
    all_gather x1, waiting for transfers between devices: 105 us -> 3.46 us  [body(): ffn_weights = lax.all_gather(ffn_pack, AXES, axis=0, tiled=True)]
    reduce_scatter x0 -> x1, waiting for transfers between devices: none -> 89.4 us  [body(): lax.psum_scatter(outer_grad, AXES, scatter_dimension=0, tiled=True)]
    ppermute x20 -> x3, waiting for transfers between devices: 92.2 us -> 11.8 us  [swap_near(): return lax.ppermute(value, 'near', [(0, 1), (1, 0)])]
    all_to_all x0 -> x1, blocking collectives: none -> 73.8 us  [exchange(): return lax.all_to_all(value, CHIPS, 0, 0, tiled=True)]
    unnamed x30 -> x46, local copies, waits for them, and re-layouts: 32 us -> 4.16 us
    slice x10 -> x0, local copies, waits for them, and re-layouts: 22.2 us -> none  [the longest x1 8.16 us: body(): full[:, 8 * D:12 * D].reshape(devices, own, CHUNKS, D).transpose(0, 2, 1, 3)]
    add x18 -> x0, other arithmetic: 19.8 us -> none  [the longest x2 14.3 us: reduce_rows(): total = keep + flip(give, 'narrow', 0, sizes['narrow']).astype(F32)]
    ppermute x20 -> x3, starting transfers between devices: 18.1 us -> 0.33 us  [swap_near(): return lax.ppermute(value, 'near', [(0, 1), (1, 0)])]
  transfers between devices with their start and end apart: 21 -> 7, of which waited for: 18 -> 6; matrix products, arithmetic and copies ran while one was open for 12% -> 7% of each run, Pallas kernels for 6% -> 16%
where the time goes in v2:
time: 386 us; the launch traced here: 385 us
  Pallas kernels  126 us (33%)
  waiting for transfers between devices  107 us (28%)
  blocking collectives  73.8 us (19%)
  local copies, waits for them, and re-layouts  30.8 us (8%)
  starting transfers between devices  16.4 us (4%)
  other arithmetic  15.8 us (4%)
  between operations  15.1 us (4%)
    reduce_scatter x1, waiting for transfers between devices, body(): lax.psum_scatter(outer_grad, AXES, scatter_dimension=0, tiled=True)  89.4 us
    all_to_all x1, blocking collectives, exchange(): return lax.all_to_all(value, CHIPS, 0, 0, tiled=True)  73.8 us
    pallas_call x1, Pallas kernels, feed_forward(): pl.pallas_call(ffn_kernel, grid=(count // rows,), in_specs=[narrow, narro...  43.3 us
    pallas_call x1, Pallas kernels, heads_backward(): pl.pallas_call(partial(by_blocks, backward_block), grid_spec=pltpu.Prefet...  18.2 us
    all_to_all x2, starting transfers between devices, exchange(): return lax.all_to_all(value, CHIPS, 0, 0, tiled=True)  16 us
    pallas_call x1, Pallas kernels, heads_forward(): pl.pallas_call(partial(by_blocks, forward_block), grid_spec=pltpu.Prefetc...  13.7 us
    pallas_call x1, Pallas kernels, attn_weight_grads(): pl.pallas_call(attn_weights_kernel, grid=(D // rows,), in_specs=[narrow,...  12.8 us
    ppermute x3, waiting for transfers between devices, swap_near(): return lax.ppermute(value, 'near', [(0, 1), (1, 0)])  11.8 us
  transfers between devices with their start and end apart: 7, of which 6 were waited for; matrix products, arithmetic and copies ran while one was open for 7% of the time, Pallas kernels for 16%

profile of v2, /device:TPU:0, one launch (start us, length us, event | category | flops | bytes accessed | tf_op | source)
XLA Modules:
  0.0 384.9 jit_solution(15074142116408597688)
XLA Ops:
  12.4 73.8 %all_to_all.15 = bf16[16,24,2432]{2,1,0:T(8,128)(2,1)S(1)} all-to-all(bf16[16,24,2432]{2,1,0:T(8,128)(2,1)S(1)} %broadcast_in_dim.24), channel_id=1, replica_groups=mesh['hi'=4,'lo'=2,'far'=2,'near'=2] {'hi','lo','far'}, dimensions={0} | all-to-all | bytes 3735552 | tf_op jit(solution)/shard_map/all_to_all | solution.py:441
  87.4 3.5 collective-permute-done
  90.9 2.4 broadcast_select_fusion
  96.0 7.8 %project_qkv.1.refs_0_ = bf16[3,1024,768]{2,1,0:T(8,128)(2,1)} custom-call(bf16[1024,768]{1,0:T(8,128)(2,1)} %tok_ref.3, bf16[768,2432]{1,0:T(8,128)(2,1)} %bitcast.43, f32[16,768]{1,0:T(8,128)} %copy.51.b_ref.vec_ref), custom_call_target="tpu_custom_call" | custom-call | flops 3623878656 | bytes 9830400 | tf_op jit(solution)/shard_map/project_qkv/pallas_call | solution.py:63
  103.8 13.7 %heads_forward.1 = (bf16[1024,768]{1,0:T(8,128)(2,1)}, f32[2,6,2,512]{3,2,1,0:T(2,128)}) custom-call(s32[2]{0:T(128)} %broadcast_minimum_fusion.limits_ref, bf16[3,1024,768]{2,1,0:T(8,128)(2,1)} %project_qkv.1.refs_0_), custom_call_target="tpu_custom_call" | custom-call | flops 6442450944 | bytes 6291456 | tf_op jit(solution)/shard_map/heads_forward/pallas_call | solution.py:154
  117.5 3.5 all-gather.2.cloned.1.call-done.wi_ref.wout_ref.wo_ref
  121.0 43.3 %feed_forward.1 = (bf16[1024,768]{1,0:T(8,128)(2,1)}, bf16[1024,768]{1,0:T(8,128)(2,1)}, bf16[1024,3072]{1,0:T(8,128)(2,1)}, bf16[1024,768]{1,0:T(8,128)(2,1)}, ...) custom-call(bf16[1024,768]{1,0:T(8,128)(2,1)} %tok_ref.3, ...), custom_call_target="tpu_custom_call" | custom-call | flops 21743271936 | bytes 35782656 | tf_op jit(solution)/shard_map/feed_forward/pallas_call | solution.py:298
  164.2 11.0 %outer_weight_grad.1 = bf16[768,3072]{1,0:T(8,128)(2,1)} custom-call(bf16[1024,3072]{1,0:T(8,128)(2,1)} %get-tuple-element.36.a_ref, bf16[1024,768]{1,0:T(8,128)(2,1)} %get-tuple-element.37.b_ref), custom_call_target="tpu_custom_call" | custom-call | flops 4831838208 | bytes 12582912 | tf_op jit(solution)/shard_map/outer_weight_grad/pallas_call | solution.py:330
  175.2 10.4 %inner_weight_grad.1 = f32[768,3072]{1,0:T(8,128)} custom-call(bf16[1024,768]{1,0:T(8,128)(2,1)} %get-tuple-element.38.a_ref, bf16[1024,3072]{1,0:T(8,128)(2,1)} %get-tuple-element.39.b_ref), custom_call_target="tpu_custom_call" | custom-call | flops 4831838208 | bytes 17301504 | tf_op jit(solution)/shard_map/inner_weight_grad/pallas_call | solution.py:354
  185.6 2.7 fusion.3
  189.8 3.3 collective-permute-done.1
  193.1 5.2 %fusion.1 = bf16[16,24,3072]{2,1,0:T(8,128)(2,1)} fusion(bf16[16,24,3072]{2,1,0:T(8,128)(2,1)} %collective-permute-done.1, f32[16,2,24,3072]{3,2,1,0:T(8,128)} %bitcast.41, s32[]{:T(128)S(6)} %select_n.27), kind=kLoop, calls=%fused_computation.5 | loop fusion | flops 3538944 | bytes 9437188 | tf_op jit(solution)/shard_map/convert_element_type | solution.py:462
  198.3 4.2 %all-to-all-start.2 = ((bf16[16,24,3072]{2,1,0:T(8,128)(2,1)}), bf16[16,24,3072]{2,1,0:T(8,128)(2,1)S(1)}, u32[]{:S(2)}, u32[]{:S(2)}) async-start(bf16[16,24,3072]{2,1,0:T(8,128)(2,1)} %fusion.1), calls=%async_computation.2 | async-start | bytes 4718592 | tf_op jit(solution)/shard_map/all_to_all | solution.py:441
  202.5 18.2 %heads_backward.1.g_ref.gcols_ref = bf16[3,1024,768]{2,1,0:T(8,128)(2,1)} custom-call(s32[2]{0:T(128)} %broadcast_minimum_fusion.limits_ref, bf16[3,1024,768]{2,1,0:T(8,128)(2,1)} %project_qkv.1.refs_0_, bf16[1024,768]{1,0:T(8,128)(2,1)} %get-tuple-element.40.refs_1_, f32[2,6,2,512]{3,2,1,0:T(2,128)} %get-tuple-element.41.refs_2_), custom_call_target="tpu_custom_call" | custom-call | flops 16106127360 | bytes 11010048 | tf_op jit(solution)/shard_map/heads_backward/pallas_call | solution.py:182
  220.7 12.8 %attn_weight_grads.1 = f32[768,3200]{1,0:T(8,128)} custom-call(bf16[1024,768]{1,0:T(8,128)(2,1)} %tok_ref.3, bf16[1024,768]{1,0:T(8,128)(2,1)} %get-tuple-element.31.att_ref, bf16[3,1024,768]{2,1,0:T(8,128)(2,1)} %heads_backward.1.g_ref.gcols_ref, bf16[3,1024,768]{2,1,0:T(8,128)(2,1)} %heads_backward.1.g_ref.gcols_ref, ...), custom_call_target="tpu_custom_call" | custom-call | flops 4831838208 | bytes 23592960 | tf_op jit(solution)/shard_map/attn_weight_grads/pallas_call | solution.py:388
  233.5 4.2 %fusion.2 = bf16[16,24,3200]{2,1,0:T(8,128)(2,1)} fusion(f32[16,2,24,3200]{3,2,1,0:T(8,128)} %bitcast.37, s32[]{:T(128)S(6)} %select_n.28), kind=kLoop, calls=%fused_computation.9 | loop fusion | bytes 4915204 | tf_op jit(solution)/shard_map/convert_element_type | solution.py:460
  237.7 5.0 %collective-permute-done.2 = bf16[16,24,3200]{2,1,0:T(8,128)(2,1)} collective-permute-done((bf16[16,24,3200]{2,1,0:T(8,128)(2,1)}, bf16[16,24,3200]{2,1,0:T(8,128)(2,1)}, u32[]{:S(2)}, u32[]{:S(2)}) %collective-permute-start.2) | collective-permute-done | bytes 2457632 | tf_op jit(solution)/shard_map/ppermute | solution.py:437
  242.7 5.1 %fusion = bf16[16,24,3200]{2,1,0:T(8,128)(2,1)} fusion(bf16[16,24,3200]{2,1,0:T(8,128)(2,1)} %collective-permute-done.2, f32[16,2,24,3200]{3,2,1,0:T(8,128)} %bitcast.38, s32[]{:T(128)S(6)} %select_n.27), kind=kLoop, calls=%fused_computation.1 | loop fusion | flops 3686400 | bytes 9830404 | tf_op jit(solution)/shard_map/convert_element_type | solution.py:462
  251.5 11.9 %all-to-all-start.1 = ((bf16[16,24,3200]{2,1,0:T(8,128)(2,1)}), bf16[16,24,3200]{2,1,0:T(8,128)(2,1)S(1)}, u32[]{:S(2)}, u32[]{:S(2)}) async-start(bf16[16,24,3200]{2,1,0:T(8,128)(2,1)} %fusion), calls=%async_computation.1 | async-start | bytes 4915200 | tf_op jit(solution)/shard_map/all_to_all | solution.py:441
  263.4 8.7 %tokens_grad.1 = bf16[1024,768]{1,0:T(8,128)(2,1)} custom-call(f32[1024,768]{1,0:T(8,128)} %get-tuple-element.33.gf_ref, bf16[3,1024,768]{2,1,0:T(8,128)(2,1)} %heads_backward.1.g_ref.gcols_ref, bf16[768,2432]{1,0:T(8,128)(2,1)} %bitcast.44), custom_call_target="tpu_custom_call" | custom-call | flops 3623878656 | bytes 12976128 | tf_op jit(solution)/shard_map/tokens_grad/pallas_call | solution.py:414
  272.1 89.4 %reduce-scatter.2.cloned.1.call-done = bf16[24,3072]{1,0:T(8,128)(2,1)} async-done(((bf16[768,3072]{1,0:T(8,128)(2,1)}), bf16[24,3072]{1,0:T(8,128)(2,1)}) %reduce-scatter.2.cloned.1.call-update) | async-done | bytes 147472 | tf_op jit(solution)/shard_map/reduce_scatter | solution.py:493
  365.4 2.3 reshape.106
  367.6 3.8 copy.55
  371.4 4.0 %reshape.107 = f32[24,3072]{1,0:T(8,128)} reshape(f32[24,32,4,24]{3,2,1,0:T(4,128)} %copy.55) | data formatting | bytes 589824 | tf_op jit(solution)/shard_map/reshape | solution.py:520
  (83 shorter events, 19.6 us)
Async XLA Ops:
  7.2 3.8 copy-start.3
  7.2 3.9 %copy-start.9 = (bf16[24,768]{1,0:T(8,128)(2,1)S(1)}, bf16[24,768]{1,0:T(8,128)(2,1)}, u32[]{:S(2)}) copy-start(bf16[24,768]{1,0:T(8,128)(2,1)} %param.26) | copy-start | bytes 110596
  7.2 4.6 %copy-start.18 = (bf16[96]{0:T(256)(128)(2,1)S(1)}, bf16[96]{0:T(256)(128)(2,1)}, u32[]{:S(2)}) copy-start(bf16[96]{0:T(256)(128)(2,1)} %param.33) | copy-start | bytes 580
  7.2 4.7 %copy-start.10 = (bf16[24]{0:T(256)(128)(2,1)S(1)}, bf16[24]{0:T(256)(128)(2,1)}, u32[]{:S(2)}) copy-start(bf16[24]{0:T(256)(128)(2,1)} %param.27) | copy-start | bytes 148
  7.2 4.7 %copy-start.11 = (bf16[24]{0:T(256)(128)(2,1)S(1)}, bf16[24]{0:T(256)(128)(2,1)}, u32[]{:S(2)}) copy-start(bf16[24]{0:T(256)(128)(2,1)} %param.28) | copy-start | bytes 148
  7.2 4.7 %copy-start.12 = (bf16[24]{0:T(256)(128)(2,1)S(1)}, bf16[24]{0:T(256)(128)(2,1)}, u32[]{:S(2)}) copy-start(bf16[24]{0:T(256)(128)(2,1)} %param.29) | copy-start | bytes 148
  7.3 4.7 %copy-start.13 = (bf16[24]{0:T(256)(128)(2,1)S(1)}, bf16[24]{0:T(256)(128)(2,1)}, u32[]{:S(2)}) copy-start(bf16[24]{0:T(256)(128)(2,1)} %param.30) | copy-start | bytes 148
  7.3 4.7 %copy-start.14 = (bf16[24]{0:T(256)(128)(2,1)S(1)}, bf16[24]{0:T(256)(128)(2,1)}, u32[]{:S(2)}) copy-start(bf16[24]{0:T(256)(128)(2,1)} %param.31) | copy-start | bytes 148
  7.3 4.7 %copy-start.15 = (bf16[24]{0:T(256)(128)(2,1)S(1)}, bf16[24]{0:T(256)(128)(2,1)}, u32[]{:S(2)}) copy-start(bf16[24]{0:T(256)(128)(2,1)} %param.35) | copy-start | bytes 148
  7.3 4.7 %copy-start.16 = (bf16[24]{0:T(256)(128)(2,1)S(1)}, bf16[24]{0:T(256)(128)(2,1)}, u32[]{:S(2)}) copy-start(bf16[24]{0:T(256)(128)(2,1)} %param.36) | copy-start | bytes 148
  7.3 4.7 %copy-start.17 = (bf16[24]{0:T(256)(128)(2,1)S(1)}, bf16[24]{0:T(256)(128)(2,1)}, u32[]{:S(2)}) copy-start(bf16[24]{0:T(256)(128)(2,1)} %param.37) | copy-start | bytes 148
  7.3 4.9 %copy-start.8 = (bf16[24,768]{1,0:T(8,128)(2,1)S(1)}, bf16[24,768]{1,0:T(8,128)(2,1)}, u32[]{:S(2)}) copy-start(bf16[24,768]{1,0:T(8,128)(2,1)} %param.23) | copy-start | bytes 110596
  7.3 4.9 %copy-start.7 = (bf16[24,768]{1,0:T(8,128)(2,1)S(1)}, bf16[24,768]{1,0:T(8,128)(2,1)}, u32[]{:S(2)}) copy-start(bf16[24,768]{1,0:T(8,128)(2,1)} %param.24) | copy-start | bytes 110596
  7.3 4.9 %copy-start.6 = (bf16[24,768]{1,0:T(8,128)(2,1)S(1)}, bf16[24,768]{1,0:T(8,128)(2,1)}, u32[]{:S(2)}) copy-start(bf16[24,768]{1,0:T(8,128)(2,1)} %param.25) | copy-start | bytes 110596
  7.3 113.6 %all-gather.2.cloned.1.call-start = ((), (), s32[]{:S(2)}) async-start(), calls=%async_computation.4 | async-start | bytes 10948608 | tf_op jit(solution)/shard_map/all_gather | solution.py:473
  12.2 74.7 %copy-start.19 = (s32[2]{0:T(128)S(1)}, s32[2]{0:T(128)}, u32[]{:S(2)}) copy-start(s32[2]{0:T(128)} %param.21) | copy-start | bytes 28
  86.2 4.7 %collective-permute-start = (bf16[16,24,2432]{2,1,0:T(8,128)(2,1)S(1)}, bf16[16,24,2432]{2,1,0:T(8,128)(2,1)}, u32[]{:S(2)}, u32[]{:S(2)}) collective-permute-start(bf16[16,24,2432]{2,1,0:T(8,128)(2,1)S(1)} %all_to_all.15), channel_id=1, source_target_pairs={{0,1},{1,0},{2,3},{3,2},{4,5},{5,4},{6,7},{7,6},{8,9},{9,8},{10,11... | collective-permute-start | bytes 5603336 | tf_op jit(solution)/shard_map/ppermute | solution.py:437
  185.6 3.0 copy-start.4
  185.6 3.1 copy-start.5
  188.4 4.7 %collective-permute-start.1 = (bf16[16,24,3072]{2,1,0:T(8,128)(2,1)S(1)}, bf16[16,24,3072]{2,1,0:T(8,128)(2,1)}, u32[]{:S(2)}, u32[]{:S(2)}) collective-permute-start(bf16[16,24,3072]{2,1,0:T(8,128)(2,1)S(1)} %fusion.3), channel_id=1, source_target_pairs={{0,1},{1,0},{2,3},{3,2},{4,5},{5,4},{6,7},{7,6},{8,9},{9,8},{10,11... | collective-permute-start | bytes 7077896 | tf_op jit(solution)/shard_map/ppermute | solution.py:437
  198.3 51.8 %all-to-all-start.2 = ((bf16[16,24,3072]{2,1,0:T(8,128)(2,1)}), bf16[16,24,3072]{2,1,0:T(8,128)(2,1)S(1)}, u32[]{:S(2)}, u32[]{:S(2)}) async-start(bf16[16,24,3072]{2,1,0:T(8,128)(2,1)} %fusion.1), calls=%async_computation.2 | async-start | bytes 4718592 | tf_op jit(solution)/shard_map/all_to_all | solution.py:441
  202.5 159.0 %reduce-scatter.2.cloned.1.call-start = ((), (), s32[]{:S(2)}) async-start(), calls=%async_computation.5 | async-start | bytes 4866048 | tf_op jit(solution)/shard_map/reduce_scatter | solution.py:493
  237.7 5.0 %collective-permute-start.2 = (bf16[16,24,3200]{2,1,0:T(8,128)(2,1)}, bf16[16,24,3200]{2,1,0:T(8,128)(2,1)}, u32[]{:S(2)}, u32[]{:S(2)}) collective-permute-start(bf16[16,24,3200]{2,1,0:T(8,128)(2,1)} %fusion.2), channel_id=1, source_target_pairs={{0,1},{1,0},{2,3},{3,2},{4,5},{5,4},{6,7},{7,6},{8,9},{9,8},{10,11... | collective-permute-start | bytes 7372808 | tf_op jit(solution)/shard_map/ppermute | solution.py:437
  251.5 123.9 %all-to-all-start.1 = ((bf16[16,24,3200]{2,1,0:T(8,128)(2,1)}), bf16[16,24,3200]{2,1,0:T(8,128)(2,1)S(1)}, u32[]{:S(2)}, u32[]{:S(2)}) async-start(bf16[16,24,3200]{2,1,0:T(8,128)(2,1)} %fusion), calls=%async_computation.1 | async-start | bytes 4915200 | tf_op jit(solution)/shard_map/all_to_all | solution.py:441
  (3 other events, 4.0 us)
Sparse Core Ops, SparseCore 0:
  12.0 108.9 all-gather.1
  237.9 123.5 reduce-scatter.1
